TPU v7x, 32 devices: a whole 2x2x4 slice. The times are simulated.
32 devices in a mesh: groups: 2 (over y), ctx: 4 (over z), head: 4 (over x, core).
Axes of the slice: x: 2, y: 2, z: 4, core: 2. Of those that a mesh axis runs over, the one named last changes fastest.
Arguments:
- queries: bfloat16 [64, 128, 576], P(('groups', 'ctx'), 'head'), parts along dimension 0, may hold values from -1024 to 1024
- out_grad: bfloat16 [64, 128, 512], P(('groups', 'ctx'), 'head'), parts along dimension 0, may hold values from -6 to 6
- latents: bfloat16 [32, 1024, 576], P(None, ('groups', 'ctx', 'head')), parts along dimension 1, may hold values from -16 to 16
- index_keys: bfloat16 [32, 1024, 128], P(None, ('groups', 'ctx', 'head')), parts along dimension 1, may hold values from -16 to 16
- index_queries: bfloat16 [64, 64, 128], P(('groups', 'ctx'), 'head'), parts along dimension 0, may hold values from -256 to 256
- index_weights: float32 [64, 64], P(('groups', 'ctx'), 'head'), parts along dimension 0, may hold values from -1 to 1
- picked_blocks: int32 [64, 4], P(('groups', 'ctx')), parts along dimension 0, may hold values from -1 to 127, as said below
- key_reach: int32 [32768], P('groups'), parts along dimension 0, may hold values from 1 to 16384, as said below
Outputs:
- query_grad: bfloat16 [64, 128, 576], P(('groups', 'ctx'), 'head'), parts along dimension 0
- latent_grad: float32 [32, 1024, 576], P(None, ('groups', 'ctx', 'head')), parts along dimension 1
- index_query_grad: bfloat16 [64, 64, 128], P(('groups', 'ctx'), 'head'), parts along dimension 0
- index_weight_grad: float32 [64, 64], P(('groups', 'ctx'), 'head'), parts along dimension 0
- index_key_grad: float32 [32, 1024, 128], P(None, ('groups', 'ctx', 'head')), parts along dimension 1
There are 2 independent parts, one for each index of `groups`. A program takes and returns all parts, laid end to end along the dimension named above; each array names one. Nothing has to cross between parts.
Inputs may be any that keep to these rules, and one draw needn't show every extreme that they name: `picked_blocks`: each row lists distinct key blocks (block b covers positions b * 128 to b * 128 + 127): first the block of the row's own query position, then blocks that lie wholly before it; -1 marks unused entries, which come only after all used ones. Among the rows of one device (aligned blocks of 8 rows) no two different blocks leave the same remainder modulo 128 // 32. key_reach[p] is the end (exclusive) of the subtree of the tree node that holds position p, nodes packed in depth-first order: p < key_reach[p], and the ranges from p to key_reach[p] of any two positions are nested or disjoint.
All inputs are finite; a program needn't handle non-finite values.
Results may differ from a plain program's by a relative error of at most 0.0049.
Values may be sent and summed in bfloat16 or wider, within the bound.
A program may use at most 256 MiB of HBM per device.

v0:
```python
import jax
import jax.numpy as jnp
from jax import lax
from jax.sharding import PartitionSpec as P

HEADS = 128
QK_DIM = 192


SCORE_FLOOR = -1e30


def masked_softmax(scores, visible):
    highest = jnp.max(jnp.where(visible, scores, SCORE_FLOOR), axis=-1, keepdims=True)
    weights = jnp.where(visible, jnp.exp(jnp.where(visible, scores - highest, 0.0)), 0.0)
    return weights / jnp.sum(weights, axis=-1, keepdims=True)


def serve_blocks(latents, index_keys, requested):
    chosen = jnp.clip(requested, 0, latents.shape[0] - 1)
    keep_mask = (requested >= 0)[:, None, None]
    latent_part = jnp.where(keep_mask, jnp.take(latents, chosen, axis=0), 0)
    index_part = jnp.where(keep_mask, jnp.take(index_keys, chosen, axis=0), 0)
    return (latent_part, index_part)


def shards(
    queries, out_grad, latents, index_keys, index_queries, index_weights, picked_blocks, key_reach
):
    owner_total = lax.axis_size("ctx")
    head_total = lax.axis_size("head")
    row_count, local_heads, key_width = queries.shape
    own_count, shard_rows = (latents.shape[0], latents.shape[1])
    index_width = index_keys.shape[2]
    block_rows = shard_rows * head_total
    context = key_reach.shape[0]
    first_pos = context - row_count * owner_total + lax.axis_index("ctx") * row_count
    places = first_pos + jnp.arange(row_count, dtype=jnp.int32)
    usable = picked_blocks >= 0
    owner_ids = jnp.arange(owner_total, dtype=jnp.int32)
    pick_owner = jnp.where(usable, picked_blocks % owner_total, 0)
    rounds = jnp.where(usable, picked_blocks // owner_total, -1)
    matches = (pick_owner[:, :, None] == owner_ids) & usable[:, :, None]
    wanted = jnp.max(jnp.where(matches, rounds[:, :, None], -1), axis=(0, 1))
    requested = lax.all_to_all(
        jnp.repeat(wanted, head_total)[:, None],
        ("ctx", "head"),
        split_axis=0,
        concat_axis=0,
        tiled=True,
    )[:, 0]
    sent_latent, sent_index = serve_blocks(latents, index_keys, requested)
    got_latent, got_index = (
        lax.all_to_all(sent_latent, ("ctx", "head"), split_axis=0, concat_axis=0, tiled=True),
        lax.all_to_all(sent_index, ("ctx", "head"), split_axis=0, concat_axis=0, tiled=True),
    )
    got_latent = got_latent.reshape(owner_total, block_rows, key_width)
    got_index = got_index.reshape(owner_total, block_rows, index_width)
    requested_by = requested.reshape(owner_total, head_total)[:, 0]
    slot_pos = (jnp.maximum(wanted, 0) * owner_total + owner_ids)[
        :, None
    ] * block_rows + jnp.arange(block_rows, dtype=jnp.int32)[None, :]
    slot_reach = jnp.take(key_reach, slot_pos, axis=0)
    score_scale = QK_DIM ** (-0.5)
    group_rows = min(row_count, 8)
    key_count = picked_blocks.shape[1] * block_rows
    latent_acc = jnp.zeros((owner_total, block_rows, key_width), jnp.float32)
    index_acc = jnp.zeros((owner_total, block_rows, index_width), jnp.float32)
    query_parts, masses, index_parts, saved_parts = ([], [], [], [])
    flat_slots = pick_owner.reshape(-1)
    gathered = jnp.take(got_latent, flat_slots, axis=0).reshape(group_rows, key_count, key_width)
    gathered_index = jnp.take(got_index, flat_slots, axis=0).reshape(
        group_rows, key_count, index_width
    )
    key_pos = jnp.take(slot_pos, flat_slots, axis=0).reshape(group_rows, key_count)
    key_ends = jnp.take(slot_reach, flat_slots, axis=0).reshape(group_rows, key_count)
    place_rows = places[:, None]
    visible = (
        jnp.repeat(usable, block_rows, axis=1) & (key_pos <= place_rows) & (place_rows < key_ends)
    )
    padded_grad = jnp.pad(out_grad, ((0, 0), (0, 0), (0, key_width - out_grad.shape[2])))
    stacked = jnp.concatenate([queries, padded_grad], axis=1)
    products = jnp.einsum("gad,gkd->gak", stacked, gathered, preferred_element_type=jnp.float32)
    attention = masked_softmax(products[:, :local_heads] * score_scale, visible[:, None, :])
    value_pull = products[:, local_heads:]
    row_inner = jnp.sum(attention * value_pull, axis=-1, keepdims=True)
    score_grad = (score_scale * attention * (value_pull - row_inner)).astype(jnp.bfloat16)
    attention_low = attention.astype(jnp.bfloat16)
    query_parts.append(
        jnp.einsum("ghk,gkd->ghd", score_grad, gathered, preferred_element_type=jnp.float32).astype(
            jnp.bfloat16
        )
    )
    coeffs = jnp.concatenate([score_grad, attention_low], axis=1)
    key_grad = jnp.einsum("gak,gad->gkd", coeffs, stacked, preferred_element_type=jnp.float32)
    latent_acc = latent_acc.at[flat_slots].add(key_grad.reshape(-1, block_rows, key_width))
    masses.append(jnp.sum(attention, axis=1))
    index_score = jnp.einsum(
        "ghd,gkd->ghk", index_queries, gathered_index, preferred_element_type=jnp.float32
    )
    weight_rows = index_weights
    index_parts.append(jnp.sum(weight_rows[:, :, None] * jnp.maximum(index_score, 0.0), axis=1))
    saved_parts.append((flat_slots, gathered_index, visible, index_score))
    mass_total, logit_total = lax.psum((masses[0], index_parts[0]), "head")
    target = mass_total / HEADS
    index_query_parts, weight_parts = ([], [])
    for number, (flat_slots, gathered_index, visible, index_score) in enumerate(saved_parts):
        index_probs = masked_softmax(logit_total, visible)
        logit_grad = index_probs - target
        weight_rows = index_weights
        positive = jnp.maximum(index_score, 0.0)
        weight_parts.append(jnp.sum(logit_grad[:, None, :] * positive, axis=-1))
        spread = jnp.where(
            index_score > 0.0, logit_grad[:, None, :] * weight_rows[:, :, None], 0.0
        ).astype(jnp.bfloat16)
        index_query_parts.append(
            jnp.einsum(
                "ghk,gkd->ghd", spread, gathered_index, preferred_element_type=jnp.float32
            ).astype(jnp.bfloat16)
        )
        index_grad = jnp.einsum(
            "ghk,ghd->gkd", spread, index_queries, preferred_element_type=jnp.float32
        )
        index_acc = index_acc.at[flat_slots].add(index_grad.reshape(-1, block_rows, index_width))
    back_latent, back_index = (
        lax.all_to_all(
            latent_acc.reshape(owner_total * head_total, shard_rows, key_width),
            ("ctx", "head"),
            split_axis=0,
            concat_axis=0,
            tiled=True,
        ),
        lax.all_to_all(
            index_acc.reshape(owner_total * head_total, shard_rows, index_width),
            ("ctx", "head"),
            split_axis=0,
            concat_axis=0,
            tiled=True,
        ),
    )
    senders = jnp.repeat(requested_by, head_total)
    home_rows = jnp.clip(senders, 0, own_count - 1)
    latent_grad = (
        jnp.zeros((own_count, shard_rows, key_width), jnp.float32).at[home_rows].add(back_latent)
    )
    index_key_grad = (
        jnp.zeros((own_count, shard_rows, index_width), jnp.float32).at[home_rows].add(back_index)
    )
    return (query_parts[0], latent_grad, index_query_parts[0], weight_parts[0], index_key_grad)


def solution(mesh):
    placed = (
        P(("groups", "ctx"), "head", None),
        P(("groups", "ctx"), "head", None),
        P(None, ("groups", "ctx", "head"), None),
        P(None, ("groups", "ctx", "head"), None),
        P(("groups", "ctx"), "head", None),
        P(("groups", "ctx"), "head"),
        P(("groups", "ctx"), None),
        P("groups"),
    )
    return jax.shard_map(
        shards,
        mesh=mesh,
        in_specs=placed,
        out_specs=(
            P(("groups", "ctx"), "head", None),
            P(None, ("groups", "ctx", "head"), None),
            P(("groups", "ctx"), "head", None),
            P(("groups", "ctx"), "head"),
            P(None, ("groups", "ctx", "head"), None),
        ),
        check_vma=False,
    )
```

profile of v0, /device:TPU:11, one launch (start us, length us, event | category | flops | bytes accessed | tf_op | source)
XLA Modules:
  0.0 196.8 jit_solution(16300401946255734426)
XLA Ops:
  0.7 0.8 fusion.29
  1.5 0.7 compare_and_fusion.2
  2.4 0.7 all_to_all.24
  3.0 6.6 %all-to-all-start = ((s32[16,1,1]{2,1,0:T(1,128)}), s32[16,1,1]{2,1,0:T(1,128)S(1)}, u32[]{:S(2)}, u32[]{:S(2)}) async-start(s32[16,1,1]{2,1,0:T(1,128)} %all_to_all.24), calls=%async_computation | async-start | bytes 16384 | tf_op jit(solution)/shard_map/all_to_all | solution.py:45
  10.0 3.5 %gather_fusion = s32[512]{0:T(512)S(1)} fusion(s32[16384]{0:T(1024)} %param.17, s32[1024]{0:T(1024)S(1)} %pad_clamp_fusion.2), kind=kCustom, calls=%fused_computation.2 | custom fusion | bytes 6144 | tf_op jit(solution)/shard_map/jit(_take)/gather | solution.py:63
  13.6 0.6 gather_fusion.5
  14.1 0.6 gather_fusion.6
  14.8 0.7 fusion.47
  15.5 0.7 gather_fusion.1
  16.2 0.6 gather_fusion.3
  16.8 0.4 compare_reduce_fusion
  17.2 0.8 select_select_fusion.1
  17.9 6.0 %all-to-all-start.3 = ((bf16[16,32,128]{2,1,0:T(8,128)(2,1)}), bf16[16,32,128]{2,1,0:T(8,128)(2,1)S(1)}, u32[]{:S(2)}, u32[]{:S(2)}) async-start(bf16[16,32,128]{2,1,0:T(8,128)(2,1)} %select_select_fusion.1), calls=%async_computation.3 | async-start | bytes 262144 | tf_op jit(solution)/shard_map/all_to_all | solution.py:55
  23.9 1.0 select_select_fusion
  25.0 4.1 %all-to-all-done.3 = bf16[16,32,128]{2,1,0:T(8,128)(2,1)S(1)} async-done(((bf16[16,32,128]{2,1,0:T(8,128)(2,1)}), bf16[16,32,128]{2,1,0:T(8,128)(2,1)S(1)}, u32[]{:S(2)}, u32[]{:S(2)}) %all-to-all-start.3) | async-done | bytes 131104 | tf_op jit(solution)/shard_map/all_to_all | solution.py:55
  29.1 6.3 %all-to-all-start.1 = ((bf16[16,32,576]{2,1,0:T(8,128)(2,1)}), bf16[16,32,576]{2,1,0:T(8,128)(2,1)S(1)}, u32[]{:S(2)}, u32[]{:S(2)}) async-start(bf16[16,32,576]{2,1,0:T(8,128)(2,1)} %select_select_fusion), calls=%async_computation.1 | async-start | bytes 1310720 | tf_op jit(solution)/shard_map/all_to_all | solution.py:54
  35.6 0.7 gather_fusion.4
  36.4 0.7 bitcast_select_fusion
  37.1 0.4 multiply_reduce_fusion.2
  37.5 14.3 %all-to-all-done.1 = bf16[16,32,576]{2,1,0:T(8,128)(2,1)S(1)} async-done(((bf16[16,32,576]{2,1,0:T(8,128)(2,1)}), bf16[16,32,576]{2,1,0:T(8,128)(2,1)S(1)}, u32[]{:S(2)}, u32[]{:S(2)}) %all-to-all-start.1) | async-done | bytes 589856 | tf_op jit(solution)/shard_map/all_to_all | solution.py:54
  51.9 0.3 copy.80
  52.2 3.3 %gather_fusion.2 = bf16[32,128,576]{1,2,0:T(8,128)(2,1)} fusion(bf16[4,128,576]{1,2,0:T(8,128)(2,1)S(1)} %copy.80, s32[1024]{0:T(1024)S(1)} %pad_clamp_fusion), kind=kCustom, calls=%fused_computation.4 | custom fusion | bytes 9437312 | tf_op jit(solution)/shard_map/jit(_take)/gather | solution.py:71
  55.5 7.5 %copy.81 = bf16[32,128,576]{1,0,2:T(8,128)(2,1)} copy(bf16[32,128,576]{1,2,0:T(8,128)(2,1)} %gather_fusion.2) | data formatting | bytes 9437184 | tf_op jit(solution)/shard_map/jit(_take)/gather | solution.py:71
  63.0 8.6 %gather.30 = bf16[8,512,576]{1,0,2:T(8,128)(2,1)} reshape(bf16[32,128,576]{1,0,2:T(8,128)(2,1)} %copy.81) | data formatting | bytes 9437184 | tf_op jit(solution)/shard_map/jit(_take)/gather | solution.py:71
  71.6 2.8 %broadcast_select_fusion = bf16[8,512,576]{1,0,2:T(8,128)(2,1)S(1)} fusion(bf16[8,512,576]{1,0,2:T(8,128)(2,1)} %gather.30, pred[8,512]{1,0:T(8,128)(4,1)S(1)} %broadcast_bitcast_fusion), kind=kLoop, calls=%fused_computation.12 | loop fusion | flops 2359296 | bytes 9441280 | tf_op jit(solution)/shard_map/jit(_take)/select_n | solution.py:71
  74.4 2.8 %fusion.3 = f32[8,64,512]{2,1,0:T(8,128)S(1)} fusion(bf16[8,512,576]{1,0,2:T(8,128)(2,1)S(1)} %broadcast_select_fusion, bf16[8,32,512]{2,1,0:T(8,128)(2,1)S(1)} %copy-done.6, bf16[8,32,576]{2,1,0:T(8,128)(2,1)S(1)} %copy-done.5), kind=kOutput, calls=%fused_computation.15 | convolution fusion | flops 303759360 | bytes 6324224 | tf_op jit(solution)/shard_map/gad,gkd->gak/dot_general | solution.py:83
  77.2 1.5 fusion.49
  78.7 0.3 fusion.45
  78.9 10.2 %all-reduce.1 = (f32[8,512]{1,0:T(8,128)S(1)}, f32[8,512]{1,0:T(8,128)S(1)}) all-reduce(f32[8,512]{1,0:T(8,128)S(1)} %get-tuple-element.6, f32[8,512]{1,0:T(8,128)S(1)} %get-tuple-element.22), channel_id=1, replica_groups=mesh['groups'=2,'ctx'=4,'head'=4] {'head'}, use_global_device_ids=true, to_apply=%region_11.13 | all-reduce | flops 8192 | bytes 65536 | tf_op jit(solution)/shard_map/psum | solution.py:104
  89.5 2.0 %fusion.26 = f32[8,512,128]{2,1,0:T(8,128)} fusion(bf16[8,16,128]{2,1,0:T(8,128)(2,1)S(1)} %copy-done.7, f32[8,512,16]{1,2,0:T(8,128)S(1)} %get-tuple-element.23, f32[8,16]{1,0:T(8,128)S(1)} %copy-done.9, f32[8,512]{1,0:T(8,128)S(1)} %multiply_subtract_fusion), kind=kOutput, calls=%fused_computation.52 | convolution fusion | flops 17039360 | bytes 2408960 | tf_op jit(solution)/shard_map/ghk,ghd->gkd/dot_general | solution.py:121
  91.6 0.7 broadcast_in_dim.204
  92.3 6.8 %scatter_fusion.2 = f32[4,128,128]{2,1,0:T(8,128)} fusion(f32[4,128,128]{2,1,0:T(8,128)} %broadcast_in_dim.204, s32[32]{0:T(128)S(1)} %fusion.33, f32[32,128,128]{2,1,0:T(8,128)} %bitcast.40), kind=kCustom, calls=%fused_computation.9 | custom fusion | flops 524288 | bytes 6291584 | tf_op jit(solution)/shard_map/scatter-add | solution.py:124
  99.1 5.3 %all-to-all-start.4 = ((f32[16,32,128]{2,1,0:T(8,128)}), f32[16,32,128]{2,1,0:T(8,128)S(1)}, u32[]{:S(2)}, u32[]{:S(2)}) async-start(f32[16,32,128]{2,1,0:T(8,128)} %bitcast.13), calls=%async_computation.4 | async-start | bytes 524288 | tf_op jit(solution)/shard_map/all_to_all | solution.py:133
  104.4 1.2 multiply_convert_fusion
  105.6 1.4 fusion.15
  107.1 9.1 %copy.84 = f32[8,512,576]{1,0,2:T(8,128)} copy(f32[8,512,576]{1,2,0:T(8,128)S(1)} %fusion.15) | data formatting | bytes 18874368 | tf_op jit(solution)/shard_map/gak,gad->gkd/dot_general | solution.py:95
  116.2 10.8 %reshape.342 = f32[32,128,576]{1,0,2:T(8,128)} reshape(f32[8,512,576]{1,0,2:T(8,128)} %copy.84) | data formatting | bytes 18874368 | tf_op jit(solution)/shard_map/reshape | solution.py:96
  127.0 12.8 %copy.85 = f32[32,128,576]{1,2,0:T(8,128)} copy(f32[32,128,576]{1,0,2:T(8,128)} %reshape.342) | data formatting | bytes 18874368 | tf_op jit(solution)/shard_map/reshape | solution.py:96
  139.9 12.5 %scatter_fusion = f32[4,128,576]{1,2,0:T(8,128)S(1)} fusion(f32[4,128,576]{1,2,0:T(8,128)S(1)} %broadcast_in_dim.194, s32[32]{0:T(128)S(1)} %fusion.33, f32[32,128,576]{1,2,0:T(8,128)} %copy.85), kind=kCustom, calls=%fused_computation.7 | custom fusion | flops 2359296 | bytes 28311680 | tf_op jit(solution)/shard_map/scatter-add | solution.py:96
  152.4 1.5 copy.86
  153.9 6.0 %all-to-all-start.2 = ((f32[16,32,576]{2,1,0:T(8,128)}), f32[16,32,576]{2,1,0:T(8,128)}, u32[]{:S(2)}, u32[]{:S(2)}) async-start(f32[16,32,576]{2,1,0:T(8,128)} %bitcast.41), calls=%async_computation.2 | async-start | bytes 2621440 | tf_op jit(solution)/shard_map/all_to_all | solution.py:126
  160.2 0.7 multiply_reduce_fusion.1
  160.9 0.9 convolution_convert_fusion
  161.9 5.7 %fusion.10 = bf16[8,32,576]{2,1,0:T(8,128)(2,1)} fusion(bf16[8,32,512]{2,1,0:T(8,128)(2,1)S(1)} %multiply_convert_fusion, bf16[8,512,576]{1,0,2:T(8,128)(2,1)} %copy-done.2), kind=kOutput, calls=%fused_computation.23 | convolution fusion | flops 151142400 | bytes 5275648 | tf_op jit(solution)/shard_map/ghk,gkd->ghd/dot_general | solution.py:90
  167.7 1.2 scatter_fusion.3
  168.9 21.7 %all-to-all-done.2 = f32[16,32,576]{2,1,0:T(8,128)} async-done(((f32[16,32,576]{2,1,0:T(8,128)}), f32[16,32,576]{2,1,0:T(8,128)}, u32[]{:S(2)}, u32[]{:S(2)}) %all-to-all-start.2) | async-done | bytes 1179680 | tf_op jit(solution)/shard_map/all_to_all | solution.py:126
  190.5 1.8 broadcast_in_dim.192
  192.3 4.4 %scatter_fusion.1 = f32[32,32,576]{2,1,0:T(8,128)} fusion(f32[32,32,576]{2,1,0:T(8,128)} %broadcast_in_dim.192, s32[16]{0:T(128)S(1)} %fusion.34, f32[16,32,576]{2,1,0:T(8,128)} %all-to-all-done.2), kind=kCustom, calls=%fused_computation.8 | custom fusion | flops 294912 | bytes 3539008 | tf_op jit(solution)/shard_map/scatter-add | solution.py:144
  (55 shorter events, 1.8 us)
Async XLA Ops:
  0.6 14.9 %copy-start = (bf16[32,32,576]{2,1,0:T(8,128)(2,1)S(1)}, bf16[32,32,576]{2,1,0:T(8,128)(2,1)}, u32[]{:S(2)}) copy-start(bf16[32,32,576]{2,1,0:T(8,128)(2,1)} %param.12) | copy-start | bytes 3538948
  0.6 15.5 %copy-start.8 = (bf16[32,32,128]{2,1,0:T(8,128)(2,1)S(1)}, bf16[32,32,128]{2,1,0:T(8,128)(2,1)}, u32[]{:S(2)}) copy-start(bf16[32,32,128]{2,1,0:T(8,128)(2,1)} %param.13) | copy-start | bytes 786436
  3.0 11.8 %all-to-all-start = ((s32[16,1,1]{2,1,0:T(1,128)}), s32[16,1,1]{2,1,0:T(1,128)S(1)}, u32[]{:S(2)}, u32[]{:S(2)}) async-start(s32[16,1,1]{2,1,0:T(1,128)} %all_to_all.24), calls=%async_computation | async-start | bytes 16384 | tf_op jit(solution)/shard_map/all_to_all | solution.py:45
  17.9 11.2 %all-to-all-start.3 = ((bf16[16,32,128]{2,1,0:T(8,128)(2,1)}), bf16[16,32,128]{2,1,0:T(8,128)(2,1)S(1)}, u32[]{:S(2)}, u32[]{:S(2)}) async-start(bf16[16,32,128]{2,1,0:T(8,128)(2,1)} %select_select_fusion.1), calls=%async_computation.3 | async-start | bytes 262144 | tf_op jit(solution)/shard_map/all_to_all | solution.py:55
  25.0 12.1 %copy-start.7 = (bf16[8,16,128]{2,1,0:T(8,128)(2,1)S(1)}, bf16[8,16,128]{2,1,0:T(8,128)(2,1)}, u32[]{:S(2)}) copy-start(bf16[8,16,128]{2,1,0:T(8,128)(2,1)} %param.14) | copy-start | bytes 98308
  25.0 12.1 %copy-start.9 = (f32[8,16]{1,0:T(8,128)S(1)}, f32[8,16]{1,0:T(8,128)}, u32[]{:S(2)}) copy-start(f32[8,16]{1,0:T(8,128)} %param.15) | copy-start | bytes 1540
  29.1 22.7 %all-to-all-start.1 = ((bf16[16,32,576]{2,1,0:T(8,128)(2,1)}), bf16[16,32,576]{2,1,0:T(8,128)(2,1)S(1)}, u32[]{:S(2)}, u32[]{:S(2)}) async-start(bf16[16,32,576]{2,1,0:T(8,128)(2,1)} %select_select_fusion), calls=%async_computation.1 | async-start | bytes 1310720 | tf_op jit(solution)/shard_map/all_to_all | solution.py:54
  71.6 2.8 %copy-start.5 = (bf16[8,32,576]{2,1,0:T(8,128)(2,1)S(1)}, bf16[8,32,576]{2,1,0:T(8,128)(2,1)}, u32[]{:S(2)}) copy-start(bf16[8,32,576]{2,1,0:T(8,128)(2,1)} %param.10) | copy-start | bytes 884740
  71.6 2.8 %copy-start.6 = (bf16[8,32,512]{2,1,0:T(8,128)(2,1)S(1)}, bf16[8,32,512]{2,1,0:T(8,128)(2,1)}, u32[]{:S(2)}) copy-start(bf16[8,32,512]{2,1,0:T(8,128)(2,1)} %param.11) | copy-start | bytes 786436
  74.4 2.8 %copy-start.2 = (bf16[8,512,576]{1,0,2:T(8,128)(2,1)}, bf16[8,512,576]{1,0,2:T(8,128)(2,1)S(1)}, u32[]{:S(2)}) copy-start(bf16[8,512,576]{1,0,2:T(8,128)(2,1)S(1)} %broadcast_select_fusion) | copy-start | bytes 14155780
  77.2 1.5 copy-start.4
  99.1 54.8 %all-to-all-start.4 = ((f32[16,32,128]{2,1,0:T(8,128)}), f32[16,32,128]{2,1,0:T(8,128)S(1)}, u32[]{:S(2)}, u32[]{:S(2)}) async-start(f32[16,32,128]{2,1,0:T(8,128)} %bitcast.13), calls=%async_computation.4 | async-start | bytes 524288 | tf_op jit(solution)/shard_map/all_to_all | solution.py:133
  153.9 36.7 %all-to-all-start.2 = ((f32[16,32,576]{2,1,0:T(8,128)}), f32[16,32,576]{2,1,0:T(8,128)}, u32[]{:S(2)}, u32[]{:S(2)}) async-start(f32[16,32,576]{2,1,0:T(8,128)} %bitcast.41), calls=%async_computation.2 | async-start | bytes 2621440 | tf_op jit(solution)/shard_map/all_to_all | solution.py:126
  168.9 27.9 %copy-start.3 = (f32[32,32,128]{2,1,0:T(8,128)}, f32[32,32,128]{2,1,0:T(8,128)S(1)}, u32[]{:S(2)}) copy-start(f32[32,32,128]{2,1,0:T(8,128)S(1)} %scatter_fusion.3) | copy-start | bytes 1572868
  190.5 6.2 %copy-start.1 = (bf16[32,32,576]{2,1,0:T(8,128)(2,1)S(1)}, bf16[32,32,576]{2,1,0:T(8,128)(2,1)}, u32[]{:S(2)}) copy-start(bf16[32,32,576]{2,1,0:T(8,128)(2,1)} %param.12) | copy-start | bytes 3538948
where the time goes:
time: 198 us; the launch traced here: 197 us
  local copies, waits for them, and re-layouts  64.5 us (33%)
  waiting for transfers between devices  40.1 us (20%)
  other arithmetic  37.5 us (19%)
  starting transfers between devices  30.2 us (15%)
  matrix products  13.3 us (7%)
  blocking collectives  10.2 us (5%)
    reshape x2, local copies, waits for them, and re-layouts, shards(): key_grad.reshape(-1, block_rows, key_width)  23.6 us
    all_to_all x1, waiting for transfers between devices, shards(): lax.all_to_all(latent_acc.reshape(owner_total * head_total, shard_rows, k...  21.7 us
    gather x3, local copies, waits for them, and re-layouts, shards(): jnp.take(got_latent, flat_slots, axis=0)  19.4 us
    all_to_all x1, waiting for transfers between devices, shards(): lax.all_to_all(sent_latent, ('ctx', 'head'), split_axis=0, concat_axis=0,...  14.3 us
    scatter-add x1, other arithmetic, shards(): latent_acc.at[flat_slots].add(key_grad.reshape(-1, block_rows, key_width))  12.5 us
    psum x1, blocking collectives, shards(): mass_total, logit_total = lax.psum((masses[0], index_parts[0]), 'head')  10.2 us
    dot_general x1, local copies, waits for them, and re-layouts, shards(): jnp.einsum('gak,gad->gkd', coeffs, stacked, preferred_element_type=jnp.fl...  9.12 us
    scatter-add x1, other arithmetic, shards(): index_acc.at[flat_slots]  6.82 us
  transfers between devices with their start and end apart: 5, of which 3 were waited for; matrix products, arithmetic and copies ran while one was open for 34% of the time, Pallas kernels for 0%

commit v1 on v0

v1 whole, which is shorter than its diff:
```python
import functools

import jax
import jax.numpy as jnp
from jax import lax
from jax.experimental import pallas as pl
from jax.experimental.pallas import tpu as pltpu
from jax.sharding import PartitionSpec as P

HEADS = 128
QK_DIM = 192
SCORE_FLOOR = -1e30
LANES = 128
MESH = pl.DeviceIdType.MESH
VMEM_BYTES = 56 * 1024 * 1024

NT = (((1,), (1,)), ((), ()))
TN = (((0,), (0,)), ((), ()))
NN = (((1,), (0,)), ((), ()))


def dot(a, b, dims):
    return lax.dot_general(a, b, dims, preferred_element_type=jnp.float32)


def exchange_kernel(
    owners,
    heads,
    sizes,
    q_hbm,
    g_hbm,
    lat_hbm,
    key_hbm,
    iq_ref,
    iw_ref,
    pick_ref,
    reach_hbm,
    qg_ref,
    back_lat_ref,
    back_key_ref,
    iqg_ref,
    iwg_ref,
    home_ref,
    q_buf,
    g_buf,
    lat_buf,
    key_buf,
    reach_buf,
    want_buf,
    asked,
    row_send,
    rows,
    part,
    glat,
    gkey,
    rlat,
    rkey,
    hlat,
    hkey,
    local_sem,
    ask_s,
    ask_r,
    row_s,
    row_r,
    fwd_s,
    fwd_r,
    part_s,
    part_r,
    glat_s,
    glat_r,
    gkey_s,
    gkey_r,
    hlat_s,
    hlat_r,
    hkey_s,
    hkey_r,
):
    row_count, local_heads, key_width, latent_width, shard_rows, context = sizes
    key_at = -(-key_width // LANES) * LANES
    block_rows = shard_rows * heads
    shift = owners.bit_length() - 1
    me_c = lax.axis_index("ctx")
    me_h = lax.axis_index("head")

    def ctx_at(step):
        return lax.rem(me_c + step + owners, owners)

    def head_at(step):
        return lax.rem(me_h + step + heads, heads)

    def remote(src, dst, send_sem, recv_sem, **where):
        return pltpu.make_async_remote_copy(
            src_ref=src,
            dst_ref=dst,
            send_sem=send_sem,
            recv_sem=recv_sem,
            device_id=where,
            device_id_type=MESH,
        )

    loads = [
        pltpu.make_async_copy(src, dst, local_sem.at[number])
        for number, (src, dst) in enumerate(
            (
                (lat_hbm, lat_buf),
                (key_hbm, key_buf),
                (reach_hbm, reach_buf),
                (q_hbm, q_buf),
                (g_hbm, g_buf),
            )
        )
    ]
    for load in loads:
        load.start()
    barrier = pltpu.get_barrier_semaphore()
    for step in range(1, owners):
        pl.semaphore_signal(
            barrier, inc=1, device_id={"ctx": ctx_at(step)}, device_id_type=MESH
        )
    for step in range(1, heads):
        pl.semaphore_signal(
            barrier, inc=1, device_id={"head": head_at(step)}, device_id_type=MESH
        )

    lane = lax.broadcasted_iota(jnp.int32, (row_count, LANES), 1)
    picked = pick_ref[...]
    by_row = jnp.full((row_count, LANES), -1, jnp.int32)
    for number in range(picked.shape[1]):
        column = jnp.broadcast_to(picked[:, number : number + 1], (row_count, LANES))
        match = (column >= 0) & ((column & (owners - 1)) == lane)
        by_row = jnp.where(match, column >> shift, by_row)
    wanted = jnp.max(by_row, axis=0, keepdims=True)
    want_buf[...] = jnp.broadcast_to(wanted, want_buf.shape)
    pl.semaphore_wait(barrier, owners + heads - 2)

    asks = []
    for step in range(1, owners):
        copy = remote(
            want_buf,
            asked.at[step - 1],
            ask_s.at[step - 1],
            ask_r.at[step - 1],
            ctx=ctx_at(step),
        )
        copy.start()
        asks.append(copy)

    def forward(step):
        copies = []
        for turn in range(1, heads):
            slot = rows.at[ctx_at(-step), me_h]
            copy = remote(
                slot, slot, fwd_s.at[step, turn - 1], fwd_r.at[step, turn - 1], head=head_at(turn)
            )
            copy.start()
            copies.append(copy)
        return copies

    loads[0].wait()
    loads[1].wait()
    first_lane = lax.broadcasted_iota(jnp.int32, (1, LANES), 1)
    own_round = jnp.max(jnp.where(first_lane == me_c, wanted, -1))
    at = jnp.maximum(own_round, 0)
    rows[me_c, me_h, :, :key_width] = lat_buf[at]
    rows[me_c, me_h, :, key_at:] = key_buf[at]
    homes = [own_round]
    sends = list(forward(0))
    row_copies = []
    for step in range(1, owners):
        asks[step - 1].wait_recv()
        told = jnp.max(jnp.where(first_lane == me_c, asked[step - 1, 0:1, :], -1))
        homes.append(told)
        at = jnp.maximum(told, 0)
        row_send[step - 1, :, :key_width] = lat_buf[at]
        row_send[step - 1, :, key_at:] = key_buf[at]
        copy = remote(
            row_send.at[step - 1],
            rows.at[me_c, me_h],
            row_s.at[owners - step - 1],
            row_r.at[owners - step - 1],
            ctx=ctx_at(-step),
        )
        copy.start()
        row_copies.append(copy)
    home_lane = lax.broadcasted_iota(jnp.int32, home_ref.shape, 1)
    home_all = jnp.full(home_ref.shape, -1, jnp.int32)
    for step in range(owners):
        home_all = jnp.where(home_lane == step, homes[step], home_all)
    home_ref[...] = home_all

    loads[2].wait()
    first_pos = context - row_count * owners + me_c * row_count
    places = first_pos + lax.broadcasted_iota(jnp.int32, (row_count, block_rows), 0)
    offsets = lax.broadcasted_iota(jnp.int32, (row_count, block_rows), 1)
    seen = []
    for owner in range(owners):
        block = (
            jnp.maximum(jnp.max(jnp.where(first_lane == owner, wanted, -1)), 0) * owners + owner
        )
        ends = jnp.broadcast_to(reach_buf[pl.ds(block, 1), :], places.shape)
        used = jnp.broadcast_to(by_row[:, owner : owner + 1], places.shape) >= 0
        ok = used & (block * block_rows + offsets <= places) & (places < ends)
        seen.append(jnp.where(ok, 1.0, 0.0))
    visible = jnp.concatenate(seen, axis=1)
    key_count = owners * block_rows

    for step in range(1, owners):
        slot = rows.at[ctx_at(-step), me_h]
        remote(
            row_send.at[0], slot, row_s.at[step - 1], row_r.at[step - 1], ctx=ctx_at(step)
        ).wait_recv()
        sends += forward(step)
    for step in range(owners):
        for turn in range(1, heads):
            slot = rows.at[ctx_at(-step), head_at(-turn)]
            remote(
                slot, slot, fwd_s.at[step, turn - 1], fwd_r.at[step, turn - 1], head=head_at(turn)
            ).wait_recv()

    loads[3].wait()
    loads[4].wait()
    stack = row_count * local_heads
    keys = rows[:, :, :, :key_width].reshape(key_count, key_width)
    ikeys = rows[:, :, :, key_at:].reshape(key_count, rows.shape[3] - key_at)
    queries = q_buf[...].reshape(stack, key_width)
    grads = g_buf[...].reshape(stack, latent_width)
    index_heads, index_width = iq_ref.shape[1], iq_ref.shape[2]
    index_stack = row_count * index_heads
    iqueries = iq_ref[...].reshape(index_stack, index_width)
    eye = jnp.where(
        lax.broadcasted_iota(jnp.int32, (index_heads, index_heads), 0)
        == lax.broadcasted_iota(jnp.int32, (index_heads, index_heads), 1),
        1.0,
        0.0,
    )
    weights = jnp.sum(iw_ref[...][:, None, :] * eye[None], axis=2, keepdims=True)

    def softmax(scores, mask):
        held = jnp.where(mask, scores, SCORE_FLOOR)
        raised = jnp.exp(held - jnp.max(held, axis=-1, keepdims=True))
        return raised * (1.0 / jnp.sum(raised, axis=-1, keepdims=True))

    score_scale = QK_DIM ** (-0.5)
    index_score = dot(iqueries, ikeys, NT).reshape(row_count, index_heads, key_count)
    positive = jnp.maximum(index_score, 0.0)
    part[me_h, 1] = jnp.sum(weights * positive, axis=1)
    scores = dot(queries, keys, NT).reshape(row_count, local_heads, key_count) * score_scale
    attention = softmax(scores, visible[:, None, :] > 0.5)
    part[me_h, 0] = jnp.sum(attention, axis=1)
    for turn in range(1, heads):
        slot = part.at[me_h]
        copy = remote(slot, slot, part_s.at[turn - 1], part_r.at[turn - 1], head=head_at(turn))
        copy.start()
        sends.append(copy)

    pulls = dot(grads, keys[:, :latent_width], NT).reshape(row_count, local_heads, key_count)
    inner = jnp.sum(attention * pulls, axis=-1, keepdims=True)
    score_grad = (score_scale * attention * (pulls - inner)).astype(jnp.bfloat16)
    score_grad = score_grad.reshape(stack, key_count)
    low = attention.astype(jnp.bfloat16).reshape(stack, key_count)
    key_grad = dot(score_grad, queries, TN)
    value_grad = dot(low, grads, TN)
    parts4 = (owners, heads, shard_rows)
    first = (key_grad[:, :latent_width] + value_grad).astype(jnp.bfloat16)
    first = first.reshape(*parts4, latent_width)
    second = key_grad[:, latent_width:].astype(jnp.bfloat16)
    second = second.reshape(*parts4, key_width - latent_width)
    for head in range(heads):
        glat[head, :, :, :latent_width] = first[:, head]
        glat[head, :, :, latent_width:] = second[:, head]
    for turn in range(1, heads):
        copy = remote(
            glat.at[head_at(turn)],
            rlat.at[turn - 1],
            glat_s.at[turn - 1],
            glat_r.at[turn - 1],
            head=head_at(turn),
        )
        copy.start()
        sends.append(copy)
    qg_ref[...] = (
        dot(score_grad, keys, NN).astype(jnp.bfloat16).reshape(row_count, local_heads, key_width)
    )

    for turn in range(1, heads):
        slot = part.at[head_at(-turn)]
        remote(
            slot, slot, part_s.at[turn - 1], part_r.at[turn - 1], head=head_at(turn)
        ).wait_recv()
    mass, logits = part[0, 0], part[0, 1]
    for head in range(1, heads):
        mass, logits = mass + part[head, 0], logits + part[head, 1]
    logit_grad = softmax(logits, visible > 0.5) - mass * (1.0 / HEADS)
    logit_rows = logit_grad[:, None, :]
    weight_grad = jnp.sum(logit_rows * positive, axis=-1, keepdims=True)
    iwg_ref[...] = jnp.sum(weight_grad * eye[None], axis=1)
    spread = jnp.where(index_score > 0.0, logit_rows * weights, 0.0)
    spread = spread.astype(jnp.bfloat16).reshape(index_stack, key_count)
    index_grad = dot(spread, iqueries, TN).astype(jnp.bfloat16).reshape(*parts4, index_width)
    for head in range(heads):
        gkey[head] = index_grad[:, head]
    for turn in range(1, heads):
        copy = remote(
            gkey.at[head_at(turn)],
            rkey.at[turn - 1],
            gkey_s.at[turn - 1],
            gkey_r.at[turn - 1],
            head=head_at(turn),
        )
        copy.start()
        sends.append(copy)
    iqg_ref[...] = (
        dot(spread, ikeys, NN).astype(jnp.bfloat16).reshape(row_count, index_heads, index_width)
    )

    def reduce_home(own, got, out, back_ref, got_s, got_r, out_s, out_r):
        for turn in range(1, heads):
            remote(
                own.at[0],
                got.at[turn - 1],
                got_s.at[turn - 1],
                got_r.at[turn - 1],
                head=head_at(turn),
            ).wait_recv()
        mine = own.at[me_h]
        for step in range(owners):
            total = mine[ctx_at(step)].astype(jnp.float32)
            for turn in range(1, heads):
                total = total + got[turn - 1, ctx_at(step)].astype(jnp.float32)
            if step == 0:
                back_ref[0] = total.astype(jnp.bfloat16)
                continue
            out[step - 1] = total.astype(jnp.bfloat16)
            copy = remote(
                out.at[step - 1],
                back_ref.at[step],
                out_s.at[step - 1],
                out_r.at[step - 1],
                ctx=ctx_at(step),
            )
            copy.start()
            sends.append(copy)

    reduce_home(glat, rlat, hlat, back_lat_ref, glat_s, glat_r, hlat_s, hlat_r)
    reduce_home(gkey, rkey, hkey, back_key_ref, gkey_s, gkey_r, hkey_s, hkey_r)
    for out, back_ref, out_s, out_r in (
        (hlat, back_lat_ref, hlat_s, hlat_r),
        (hkey, back_key_ref, hkey_s, hkey_r),
    ):
        for step in range(1, owners):
            remote(
                out.at[step - 1],
                back_ref.at[step],
                out_s.at[step - 1],
                out_r.at[step - 1],
                ctx=ctx_at(step),
            ).wait_recv()
    for copy in asks + row_copies + sends:
        copy.wait_send()


def place_kernel(owners, home_ref, lat_ref, key_ref, lat_out, key_out):
    lat_out[...] = jnp.zeros_like(lat_out)
    key_out[...] = jnp.zeros_like(key_out)
    for step in range(owners):
        at = jnp.maximum(home_ref[0, step], 0)
        lat_out[at] = lat_out[at] + lat_ref[step].astype(jnp.float32)
        key_out[at] = key_out[at] + key_ref[step].astype(jnp.float32)


def shards(
    queries, out_grad, latents, index_keys, index_queries, index_weights, picked_blocks, key_reach
):
    owners = lax.axis_size("ctx")
    heads = lax.axis_size("head")
    row_count, local_heads, key_width = queries.shape
    latent_width = out_grad.shape[2]
    own_count, shard_rows = latents.shape[:2]
    index_width = index_keys.shape[2]
    context = key_reach.shape[0]
    block_rows = shard_rows * heads
    key_count = owners * block_rows
    wide = -(-key_width // LANES) * LANES + index_width
    sizes = (row_count, local_heads, key_width, latent_width, shard_rows, context)
    low, full, whole = jnp.bfloat16, jnp.float32, jnp.int32
    vmem = pl.BlockSpec(memory_space=pltpu.VMEM)
    anywhere = pl.BlockSpec(memory_space=pl.ANY)
    sem = pltpu.SemaphoreType.DMA
    side, turns = max(owners - 1, 1), max(heads - 1, 1)
    query_grad, back_lat, back_key, iquery_grad, weight_grad, home = pl.pallas_call(
        functools.partial(exchange_kernel, owners, heads, sizes),
        out_shape=(
            jax.ShapeDtypeStruct(queries.shape, low),
            jax.ShapeDtypeStruct((owners, shard_rows, key_width), low),
            jax.ShapeDtypeStruct((owners, shard_rows, index_width), low),
            jax.ShapeDtypeStruct(index_queries.shape, low),
            jax.ShapeDtypeStruct(index_weights.shape, full),
            jax.ShapeDtypeStruct((8, LANES), whole),
        ),
        in_specs=[anywhere, anywhere, anywhere, anywhere, vmem, vmem, vmem, anywhere],
        out_specs=(vmem,) * 6,
        scratch_shapes=[
            pltpu.VMEM(queries.shape, low),
            pltpu.VMEM(out_grad.shape, low),
            pltpu.VMEM(latents.shape, low),
            pltpu.VMEM(index_keys.shape, low),
            pltpu.VMEM((context // block_rows, block_rows), whole),
            pltpu.VMEM((8, LANES), whole),
            pltpu.VMEM((side, 8, LANES), whole),
            pltpu.VMEM((side, shard_rows, wide), low),
            pltpu.VMEM((owners, heads, shard_rows, wide), low),
            pltpu.VMEM((heads, 2, row_count, key_count), full),
            pltpu.VMEM((heads, owners, shard_rows, key_width), low),
            pltpu.VMEM((heads, owners, shard_rows, index_width), low),
            pltpu.VMEM((turns, owners, shard_rows, key_width), low),
            pltpu.VMEM((turns, owners, shard_rows, index_width), low),
            pltpu.VMEM((side, shard_rows, key_width), low),
            pltpu.VMEM((side, shard_rows, index_width), low),
            sem((5,)),
            sem((side,)),
            sem((side,)),
            sem((side,)),
            sem((side,)),
            sem((owners, turns)),
            sem((owners, turns)),
            sem((turns,)),
            sem((turns,)),
            sem((turns,)),
            sem((turns,)),
            sem((turns,)),
            sem((turns,)),
            sem((side,)),
            sem((side,)),
            sem((side,)),
            sem((side,)),
        ],
        compiler_params=pltpu.CompilerParams(
            collective_id=0, has_side_effects=True, vmem_limit_bytes=VMEM_BYTES
        ),
        name="exchange",
    )(
        queries,
        out_grad,
        latents,
        index_keys,
        index_queries,
        index_weights,
        picked_blocks,
        key_reach.reshape(context // block_rows, block_rows),
    )
    latent_grad, index_key_grad = pl.pallas_call(
        functools.partial(place_kernel, owners),
        out_shape=(
            jax.ShapeDtypeStruct((own_count, shard_rows, key_width), full),
            jax.ShapeDtypeStruct((own_count, shard_rows, index_width), full),
        ),
        in_specs=[pl.BlockSpec(memory_space=pltpu.SMEM), vmem, vmem],
        out_specs=(vmem, vmem),
        compiler_params=pltpu.CompilerParams(vmem_limit_bytes=VMEM_BYTES),
        name="place",
    )(home, back_lat, back_key)
    return (query_grad, latent_grad, iquery_grad, weight_grad, index_key_grad)


def solution(mesh):
    placed = (
        P(("groups", "ctx"), "head", None),
        P(("groups", "ctx"), "head", None),
        P(None, ("groups", "ctx", "head"), None),
        P(None, ("groups", "ctx", "head"), None),
        P(("groups", "ctx"), "head", None),
        P(("groups", "ctx"), "head"),
        P(("groups", "ctx"), None),
        P("groups"),
    )
    return jax.shard_map(
        shards,
        mesh=mesh,
        in_specs=placed,
        out_specs=(
            P(("groups", "ctx"), "head", None),
            P(None, ("groups", "ctx", "head"), None),
            P(("groups", "ctx"), "head", None),
            P(("groups", "ctx"), "head"),
            P(None, ("groups", "ctx", "head"), None),
        ),
        check_vma=False,
    )
```

time: 198 us -> 46.5 us (0.23)
  the two profiles are of different devices: /device:TPU:11 before, /device:TPU:0 now
where the time goes in v1:
time: 46.5 us; the launch traced here: 46 us
  Pallas kernels  39.6 us (85%)
  local copies, waits for them, and re-layouts  5.72 us (12%)
  between operations  0.64 us (1%)
    pallas_call x1, Pallas kernels, shards(): pl.pallas_call(functools.partial(exchange_kernel, owners, heads, sizes),...  36.8 us
    unnamed x4, local copies, waits for them, and re-layouts  5.72 us
    pallas_call x1, Pallas kernels, shards(): pl.pallas_call(functools.partial(place_kernel, owners), out_shape=(jax.Sh...  2.82 us

profile of v1, /device:TPU:0, one launch (start us, length us, event | category | flops | bytes accessed | tf_op | source)
XLA Modules:
  0.0 46.0 jit_solution(3139381887189498430)
XLA Ops:
  0.6 1.3 %copy.13.pick_ref = s32[8,4]{1,0:T(8,128)} copy(s32[8,4]{0,1:T(4,128)} %param.14) | data formatting | bytes 256 | tf_op args[6]
  2.0 36.8 %exchange.1 = (bf16[8,32,576]{2,1,0:T(8,128)(2,1)}, bf16[4,32,576]{2,1,0:T(8,128)(2,1)}, bf16[4,32,128]{2,1,0:T(8,128)(2,1)}, bf16[8,16,128]{2,1,0:T(8,128)(2,1)}, f32[8,16]{1,0:T(8,128)}, /*index=5*/s32[8,128]{1,0:T(8,128)}) custom-call(bf16[8,32,576]{2,1,0:T(8,128)(2,1)} %q_hbm.1, bf16[8,32,512]{2,1,0:T(8,128)(2,1)} %g_hbm.1, ...), custom_call_target="tpu_custom_call" | custom-call | tf_op jit(solution)/shard_map/exchange/pallas_call | solution.py:390
  38.8 2.8 %place.1 = (f32[32,32,576]{2,1,0:T(8,128)}, f32[32,32,128]{2,1,0:T(8,128)}) custom-call(s32[8,128]{1,0:T(8,128)} %get-tuple-element.14.home_ref, bf16[4,32,576]{2,1,0:T(8,128)(2,1)} %get-tuple-element.15.lat_ref, bf16[4,32,128]{2,1,0:T(8,128)(2,1)} %get-tuple-element.16.key_ref), custom_call_target="tpu_custom_call" | custom-call | tf_op jit(solution)/shard_map/place/pallas_call | solution.py:451
  41.6 1.7 %copy.17 = bf16[8,32,576]{2,1,0:T(8,128)(2,1)} copy(bf16[8,32,576]{2,1,0:T(8,128)(2,1)} %get-tuple-element.26) | data formatting | bytes 589824
  43.3 1.4 %copy.18 = bf16[8,16,128]{2,1,0:T(8,128)(2,1)} copy(bf16[8,16,128]{2,1,0:T(8,128)(2,1)} %get-tuple-element.28) | data formatting | bytes 65536
  44.7 1.3 %copy.19 = f32[8,16]{1,0:T(8,128)} copy(f32[8,16]{1,0:T(8,128)} %get-tuple-element.29) | data formatting | bytes 1024

commit v2 on v1

v2 whole, which is shorter than its diff:
```python
import functools

import jax
import jax.numpy as jnp
from jax import lax
from jax.experimental import pallas as pl
from jax.experimental.pallas import tpu as pltpu
from jax.sharding import PartitionSpec as P

HEADS = 128
QK_DIM = 192
SCORE_FLOOR = -1e30
LANES = 128
MESH = pl.DeviceIdType.MESH
VMEM_BYTES = 56 * 1024 * 1024

NT = (((1,), (1,)), ((), ()))
TN = (((0,), (0,)), ((), ()))
NN = (((1,), (0,)), ((), ()))


def dot(a, b, dims):
    return lax.dot_general(a, b, dims, preferred_element_type=jnp.float32)


def exchange_kernel(
    owners,
    heads,
    sizes,
    q_hbm,
    g_hbm,
    lat_hbm,
    key_hbm,
    iq_ref,
    iw_ref,
    pick_ref,
    reach_hbm,
    qg_ref,
    back_lat_ref,
    back_key_ref,
    iqg_ref,
    iwg_ref,
    home_ref,
    q_buf,
    g_buf,
    lat_buf,
    key_buf,
    reach_buf,
    want_buf,
    asked,
    row_send,
    rows,
    part,
    glat,
    gkey,
    near_lat,
    near_key,
    mid_lat,
    mid_key,
    far_lat,
    far_key,
    hlat,
    hkey,
    local_sem,
    ask_s,
    ask_r,
    row_s,
    row_r,
    fwd_s,
    fwd_r,
    part_s,
    part_r,
    near_s,
    near_r,
    mid_s,
    mid_r,
    hlat_s,
    hlat_r,
    hkey_s,
    hkey_r,
):
    row_count, local_heads, key_width, latent_width, shard_rows, context = sizes
    key_at = -(-key_width // LANES) * LANES
    block_rows = shard_rows * heads
    shift = owners.bit_length() - 1
    me_c = lax.axis_index("ctx")
    me_h = lax.axis_index("head")
    my_x, my_core = me_h // 2, lax.rem(me_h, 2)
    beside = me_h + 1 - 2 * my_core
    across = lax.rem(me_h + 2, heads)
    opposite = heads - 1 - me_h
    others = (beside, across, opposite)

    def ctx_at(step):
        return lax.rem(me_c + step + owners, owners)

    def remote(src, dst, send_sem, recv_sem, **where):
        return pltpu.make_async_remote_copy(
            src_ref=src,
            dst_ref=dst,
            send_sem=send_sem,
            recv_sem=recv_sem,
            device_id=where,
            device_id_type=MESH,
        )

    sends = []

    def send(copy):
        copy.start()
        sends.append(copy)

    loads = [
        pltpu.make_async_copy(src, dst, local_sem.at[number])
        for number, (src, dst) in enumerate(
            (
                (lat_hbm, lat_buf),
                (key_hbm, key_buf),
                (reach_hbm, reach_buf),
                (q_hbm, q_buf),
                (g_hbm, g_buf),
            )
        )
    ]
    for load in loads:
        load.start()
    barrier = pltpu.get_barrier_semaphore()
    for step in range(1, owners):
        pl.semaphore_signal(
            barrier, inc=1, device_id={"ctx": ctx_at(step)}, device_id_type=MESH
        )
    for other in others:
        pl.semaphore_signal(barrier, inc=1, device_id={"head": other}, device_id_type=MESH)

    lane = lax.broadcasted_iota(jnp.int32, (row_count, LANES), 1)
    diagonal = lax.broadcasted_iota(
        jnp.int32, (row_count, row_count), 0
    ) == lax.broadcasted_iota(jnp.int32, (row_count, row_count), 1)
    by_row = jnp.full((row_count, LANES), -1, jnp.int32)
    for number in range(pick_ref.shape[0]):
        line = jnp.broadcast_to(pick_ref[number : number + 1, :], (row_count, row_count))
        column = jnp.max(jnp.where(diagonal, line, -1), axis=1, keepdims=True)
        column = jnp.broadcast_to(column, (row_count, LANES))
        match = (column >= 0) & ((column & (owners - 1)) == lane)
        by_row = jnp.where(match, column >> shift, by_row)
    wanted = jnp.max(by_row, axis=0, keepdims=True)
    want_buf[...] = jnp.broadcast_to(wanted, want_buf.shape)
    pl.semaphore_wait(barrier, owners + heads - 2)

    asks = []
    for step in range(1, owners):
        asks.append(
            remote(
                want_buf,
                asked.at[step - 1],
                ask_s.at[step - 1],
                ask_r.at[step - 1],
                ctx=ctx_at(step),
            )
        )
        send(asks[-1])

    def hand_on(step, slot_head, number, to):
        slot = rows.at[step, slot_head]
        return remote(slot, slot, fwd_s.at[step, number], fwd_r.at[step, number], head=to)

    loads[0].wait()
    loads[1].wait()
    first_lane = lax.broadcasted_iota(jnp.int32, (1, LANES), 1)
    own_round = jnp.max(jnp.where(first_lane == me_c, wanted, -1))
    at = jnp.maximum(own_round, 0)
    rows[0, me_h, :, :key_width] = lat_buf[at]
    rows[0, me_h, :, key_at:] = key_buf[at]
    homes = [own_round]
    for step in range(1, owners):
        asks[step - 1].wait_recv()
        told = jnp.max(jnp.where(first_lane == me_c, asked[step - 1, 0:1, :], -1))
        homes.append(told)
        at = jnp.maximum(told, 0)
        row_send[step - 1, :, :key_width] = lat_buf[at]
        row_send[step - 1, :, key_at:] = key_buf[at]
        send(
            remote(
                row_send.at[step - 1],
                rows.at[step, me_h],
                row_s.at[step - 1],
                row_r.at[step - 1],
                ctx=ctx_at(-step),
            )
        )
    send(hand_on(0, me_h, 0, across))
    send(hand_on(0, me_h, 1, beside))
    home_lane = lax.broadcasted_iota(jnp.int32, home_ref.shape, 1)
    home_all = jnp.full(home_ref.shape, -1, jnp.int32)
    for step in range(owners):
        home_all = jnp.where(home_lane == step, homes[step], home_all)
    home_ref[...] = home_all

    loads[2].wait()
    first_pos = context - row_count * owners + me_c * row_count
    places = first_pos + lax.broadcasted_iota(jnp.int32, (row_count, block_rows), 0)
    offsets = lax.broadcasted_iota(jnp.int32, (row_count, block_rows), 1)
    seen = []
    for step in range(owners):
        owner = ctx_at(step)
        block = (
            jnp.maximum(jnp.max(jnp.where(first_lane == owner, wanted, -1)), 0) * owners + owner
        )
        ends = jnp.broadcast_to(reach_buf[pl.ds(block, 1), :], places.shape)
        used = jnp.max(jnp.where(lane == owner, by_row, -1), axis=1, keepdims=True)
        used = jnp.broadcast_to(used, places.shape) >= 0
        ok = used & (block * block_rows + offsets <= places) & (places < ends)
        seen.append(jnp.where(ok, 1.0, 0.0))

    loads[3].wait()
    loads[4].wait()
    stack = row_count * local_heads
    queries = q_buf[...].reshape(stack, key_width)
    grads = g_buf[...].reshape(stack, latent_width)
    index_heads, index_width = iq_ref.shape[1], iq_ref.shape[2]
    index_stack = row_count * index_heads
    iqueries = iq_ref[...].reshape(index_stack, index_width)
    eye = jnp.where(
        lax.broadcasted_iota(jnp.int32, (index_heads, index_heads), 0)
        == lax.broadcasted_iota(jnp.int32, (index_heads, index_heads), 1),
        1.0,
        0.0,
    )
    weights = jnp.sum(iw_ref[...][:, None, :] * eye[None], axis=2, keepdims=True)
    score_scale = QK_DIM ** (-0.5)
    index_scores, scores, pulls = [], [], []

    def keys_of(step):
        return rows[step, :, :, :key_width].reshape(block_rows, key_width)

    def ikeys_of(step):
        return rows[step, :, :, key_at:].reshape(block_rows, index_width)

    def multiply(step):
        found = dot(iqueries, ikeys_of(step), NT).reshape(row_count, index_heads, block_rows)
        index_scores.append(found)
        part[me_h, 1, step] = jnp.sum(weights * jnp.maximum(found, 0.0), axis=1)
        keys = keys_of(step)
        found = dot(queries, keys, NT).reshape(row_count, local_heads, block_rows) * score_scale
        scores.append(jnp.where(seen[step][:, None, :] > 0.5, found, SCORE_FLOOR))
        found = dot(grads, keys[:, :latent_width], NT)
        pulls.append(found.reshape(row_count, local_heads, block_rows))

    for turn in range(owners + 2):
        if turn < owners and turn > 0:
            remote(
                row_send.at[0],
                rows.at[turn, me_h],
                row_s.at[turn - 1],
                row_r.at[turn - 1],
                ctx=ctx_at(turn),
            ).wait_recv()
            send(hand_on(turn, me_h, 0, across))
            send(hand_on(turn, me_h, 1, beside))
        if 1 <= turn <= owners:
            hand_on(turn - 1, across, 0, across).wait_recv()
            send(hand_on(turn - 1, across, 2, beside))
        if turn >= 2:
            hand_on(turn - 2, beside, 1, beside).wait_recv()
            hand_on(turn - 2, opposite, 2, beside).wait_recv()
            multiply(turn - 2)

    def share(kind):
        for number, other in enumerate(others):
            slot = part.at[me_h, kind]
            send(remote(slot, slot, part_s.at[kind, number], part_r.at[kind, number], head=other))

    def softmax(chunks):
        top = functools.reduce(jnp.maximum, chunks)
        top = jnp.max(top, axis=-1, keepdims=True)
        raised = [jnp.exp(chunk - top) for chunk in chunks]
        total = jnp.sum(functools.reduce(jnp.add, raised), axis=-1, keepdims=True)
        inverse = 1.0 / total
        return [chunk * inverse for chunk in raised]

    share(1)
    attention = softmax(scores)
    for step in range(owners):
        part[me_h, 0, step] = jnp.sum(attention[step], axis=1)
    share(0)
    inner = functools.reduce(jnp.add, [a * p for a, p in zip(attention, pulls)])
    inner = jnp.sum(inner, axis=-1, keepdims=True)
    order = [*range(1, owners), 0]
    score_grads = [None] * owners
    shape = (heads // 2, 2, shard_rows)
    for step in order:
        found = score_scale * attention[step] * (pulls[step] - inner)
        found = found.astype(jnp.bfloat16).reshape(stack, block_rows)
        score_grads[step] = found
        low = attention[step].astype(jnp.bfloat16).reshape(stack, block_rows)
        key_grad = dot(found, queries, TN)
        value_grad = dot(low, grads, TN)
        front = (key_grad[:, :latent_width] + value_grad).astype(jnp.bfloat16)
        glat[step, :, :, :, :latent_width] = front.reshape(*shape, latent_width)
        rest = key_grad[:, latent_width:].astype(jnp.bfloat16)
        glat[step, :, :, :, latent_width:] = rest.reshape(*shape, key_width - latent_width)
        send(
            remote(
                glat.at[step, :, 1 - my_core],
                near_lat.at[step],
                near_s.at[step],
                near_r.at[step],
                head=beside,
            )
        )

    for kind in range(2):
        for number, other in enumerate(others):
            slot = part.at[other, kind]
            remote(
                slot, slot, part_s.at[kind, number], part_r.at[kind, number], head=other
            ).wait_recv()

    def total_of(kind, step):
        found = part[0, kind, step]
        for head in range(1, heads):
            found = found + part[head, kind, step]
        return found

    logits = [
        jnp.where(seen[step] > 0.5, total_of(1, step), SCORE_FLOOR) for step in range(owners)
    ]
    probs = softmax(logits)
    logit_grads = [probs[step] - total_of(0, step) * (1.0 / HEADS) for step in range(owners)]

    for step in order:
        remote(
            glat.at[step, :, 0],
            near_lat.at[step],
            near_s.at[step],
            near_r.at[step],
            head=beside,
        ).wait_recv()
        total = glat[step, 1 - my_x, my_core].astype(jnp.float32)
        total = total + near_lat[step, 1 - my_x].astype(jnp.float32)
        mid_lat[step] = total.astype(jnp.bfloat16)
        send(
            remote(
                mid_lat.at[step], far_lat.at[step], mid_s.at[step], mid_r.at[step], head=across
            )
        )

    spreads = []
    for step in range(owners):
        found = jnp.where(
            index_scores[step] > 0.0, logit_grads[step][:, None, :] * weights, 0.0
        )
        found = found.astype(jnp.bfloat16).reshape(index_stack, block_rows)
        spreads.append(found)
        found = dot(found, iqueries, TN).astype(jnp.bfloat16)
        gkey[step] = found.reshape(*shape, index_width)
    send(
        remote(
            gkey.at[:, :, 1 - my_core],
            near_key,
            near_s.at[owners],
            near_r.at[owners],
            head=beside,
        )
    )
    found = jnp.zeros((stack, key_width), jnp.float32)
    for step in range(owners):
        found = found + dot(score_grads[step], keys_of(step), NN)
    qg_ref[...] = found.astype(jnp.bfloat16).reshape(row_count, local_heads, key_width)

    remote(
        gkey.at[:, :, 0], near_key, near_s.at[owners], near_r.at[owners], head=beside
    ).wait_recv()
    for step in range(owners):
        total = gkey[step, 1 - my_x, my_core].astype(jnp.float32)
        total = total + near_key[step, 1 - my_x].astype(jnp.float32)
        mid_key[step] = total.astype(jnp.bfloat16)
    send(remote(mid_key, far_key, mid_s.at[owners], mid_r.at[owners], head=across))

    found = jnp.zeros((index_stack, index_width), jnp.float32)
    weight_grad = jnp.zeros((row_count, index_heads, block_rows), jnp.float32)
    for step in range(owners):
        found = found + dot(spreads[step], ikeys_of(step), NN)
        weight_grad = weight_grad + logit_grads[step][:, None, :] * jnp.maximum(
            index_scores[step], 0.0
        )
    iqg_ref[...] = found.astype(jnp.bfloat16).reshape(row_count, index_heads, index_width)
    weight_grad = jnp.sum(weight_grad, axis=-1, keepdims=True)
    iwg_ref[...] = jnp.sum(weight_grad * eye[None], axis=1)

    def home_copy(out, back_ref, out_s, out_r, step):
        return remote(
            out.at[step - 1],
            back_ref.at[step],
            out_s.at[step - 1],
            out_r.at[step - 1],
            ctx=ctx_at(step),
        )

    lat_home = (hlat, back_lat_ref, hlat_s, hlat_r)
    key_home = (hkey, back_key_ref, hkey_s, hkey_r)

    def send_home(own, near, far, home, step):
        total = own[step, my_x, my_core].astype(jnp.float32)
        total = total + near[step, my_x].astype(jnp.float32)
        total = (total + far[step].astype(jnp.float32)).astype(jnp.bfloat16)
        if step == 0:
            home[1][0] = total
        else:
            home[0][step - 1] = total
            send(home_copy(*home, step))

    for step in order:
        remote(
            mid_lat.at[step], far_lat.at[step], mid_s.at[step], mid_r.at[step], head=across
        ).wait_recv()
        send_home(glat, near_lat, far_lat, lat_home, step)
    remote(mid_key, far_key, mid_s.at[owners], mid_r.at[owners], head=across).wait_recv()
    for step in order:
        send_home(gkey, near_key, far_key, key_home, step)
    for home in (lat_home, key_home):
        for step in range(1, owners):
            home_copy(*home, step).wait_recv()
    for copy in sends:
        copy.wait_send()


def place_kernel(
    owners,
    home_ref,
    lat_hbm,
    key_hbm,
    qg_in,
    iqg_in,
    iwg_in,
    lat_out,
    key_out,
    qg_out,
    iqg_out,
    iwg_out,
    lat_buf,
    key_buf,
    sems,
):
    copies = [
        pltpu.make_async_copy(src, dst, sems.at[number])
        for number, (src, dst) in enumerate(
            (
                (lat_hbm, lat_buf),
                (key_hbm, key_buf),
                (qg_in, qg_out),
                (iqg_in, iqg_out),
                (iwg_in, iwg_out),
            )
        )
    ]
    for copy in copies:
        copy.start()
    lat_out[...] = jnp.zeros_like(lat_out)
    key_out[...] = jnp.zeros_like(key_out)
    copies[0].wait()
    copies[1].wait()
    for step in range(owners):
        at = jnp.maximum(home_ref[0, step], 0)
        lat_out[at] = lat_out[at] + lat_buf[step].astype(jnp.float32)
        key_out[at] = key_out[at] + key_buf[step].astype(jnp.float32)
    for copy in copies[2:]:
        copy.wait()


def shards(
    queries, out_grad, latents, index_keys, index_queries, index_weights, picked_blocks, key_reach
):
    owners = lax.axis_size("ctx")
    heads = lax.axis_size("head")
    row_count, local_heads, key_width = queries.shape
    latent_width = out_grad.shape[2]
    own_count, shard_rows = latents.shape[:2]
    index_width = index_keys.shape[2]
    context = key_reach.shape[0]
    block_rows = shard_rows * heads
    wide = -(-key_width // LANES) * LANES + index_width
    sizes = (row_count, local_heads, key_width, latent_width, shard_rows, context)
    low, full, whole = jnp.bfloat16, jnp.float32, jnp.int32
    vmem = pl.BlockSpec(memory_space=pltpu.VMEM)
    anywhere = pl.BlockSpec(memory_space=pl.ANY)
    sem = pltpu.SemaphoreType.DMA
    side = owners - 1
    query_grad, back_lat, back_key, iquery_grad, weight_grad, home = pl.pallas_call(
        functools.partial(exchange_kernel, owners, heads, sizes),
        out_shape=(
            jax.ShapeDtypeStruct(queries.shape, low),
            jax.ShapeDtypeStruct((owners, shard_rows, key_width), low),
            jax.ShapeDtypeStruct((owners, shard_rows, index_width), low),
            jax.ShapeDtypeStruct(index_queries.shape, low),
            jax.ShapeDtypeStruct(index_weights.shape, full),
            jax.ShapeDtypeStruct((8, LANES), whole),
        ),
        in_specs=[anywhere, anywhere, anywhere, anywhere, vmem, vmem, vmem, anywhere],
        out_specs=(vmem,) * 6,
        scratch_shapes=[
            pltpu.VMEM(queries.shape, low),
            pltpu.VMEM(out_grad.shape, low),
            pltpu.VMEM(latents.shape, low),
            pltpu.VMEM(index_keys.shape, low),
            pltpu.VMEM((context // block_rows, block_rows), whole),
            pltpu.VMEM((8, LANES), whole),
            pltpu.VMEM((side, 8, LANES), whole),
            pltpu.VMEM((side, shard_rows, wide), low),
            pltpu.VMEM((owners, heads, shard_rows, wide), low),
            pltpu.VMEM((heads, 2, owners, row_count, block_rows), full),
            pltpu.VMEM((owners, heads // 2, 2, shard_rows, key_width), low),
            pltpu.VMEM((owners, heads // 2, 2, shard_rows, index_width), low),
            pltpu.VMEM((owners, heads // 2, shard_rows, key_width), low),
            pltpu.VMEM((owners, heads // 2, shard_rows, index_width), low),
            pltpu.VMEM((owners, shard_rows, key_width), low),
            pltpu.VMEM((owners, shard_rows, index_width), low),
            pltpu.VMEM((owners, shard_rows, key_width), low),
            pltpu.VMEM((owners, shard_rows, index_width), low),
            pltpu.VMEM((side, shard_rows, key_width), low),
            pltpu.VMEM((side, shard_rows, index_width), low),
            sem((5,)),
            sem((side,)),
            sem((side,)),
            sem((side,)),
            sem((side,)),
            sem((owners, 3)),
            sem((owners, 3)),
            sem((2, 3)),
            sem((2, 3)),
            sem((owners + 1,)),
            sem((owners + 1,)),
            sem((owners + 1,)),
            sem((owners + 1,)),
            sem((side,)),
            sem((side,)),
            sem((side,)),
            sem((side,)),
        ],
        compiler_params=pltpu.CompilerParams(
            collective_id=0, has_side_effects=True, vmem_limit_bytes=VMEM_BYTES
        ),
        name="exchange",
    )(
        queries,
        out_grad,
        latents,
        index_keys,
        index_queries,
        index_weights,
        picked_blocks.T,
        key_reach.reshape(context // block_rows, block_rows),
    )
    latent_grad, index_key_grad, query_grad, iquery_grad, weight_grad = pl.pallas_call(
        functools.partial(place_kernel, owners),
        out_shape=(
            jax.ShapeDtypeStruct((own_count, shard_rows, key_width), full),
            jax.ShapeDtypeStruct((own_count, shard_rows, index_width), full),
            jax.ShapeDtypeStruct(queries.shape, low),
            jax.ShapeDtypeStruct(index_queries.shape, low),
            jax.ShapeDtypeStruct(index_weights.shape, full),
        ),
        in_specs=[pl.BlockSpec(memory_space=pltpu.SMEM)] + [anywhere] * 5,
        out_specs=(vmem, vmem, anywhere, anywhere, anywhere),
        scratch_shapes=[
            pltpu.VMEM(back_lat.shape, low),
            pltpu.VMEM(back_key.shape, low),
            sem((5,)),
        ],
        compiler_params=pltpu.CompilerParams(vmem_limit_bytes=VMEM_BYTES),
        name="place",
    )(home, back_lat, back_key, query_grad, iquery_grad, weight_grad)
    return (query_grad, latent_grad, iquery_grad, weight_grad, index_key_grad)


def solution(mesh):
    placed = (
        P(("groups", "ctx"), "head", None),
        P(("groups", "ctx"), "head", None),
        P(None, ("groups", "ctx", "head"), None),
        P(None, ("groups", "ctx", "head"), None),
        P(("groups", "ctx"), "head", None),
        P(("groups", "ctx"), "head"),
        P(("groups", "ctx"), None),
        P("groups"),
    )
    return jax.shard_map(
        shards,
        mesh=mesh,
        in_specs=placed,
        out_specs=(
            P(("groups", "ctx"), "head", None),
            P(None, ("groups", "ctx", "head"), None),
            P(("groups", "ctx"), "head", None),
            P(("groups", "ctx"), "head"),
            P(None, ("groups", "ctx", "head"), None),
        ),
        check_vma=False,
    )
```

time: 46.5 us -> 51.1 us (1.099)
  Pallas kernels: 39.6 us -> 50.2 us
  local copies, waits for them, and re-layouts: 5.72 us -> 0 us
    pallas_call x1, Pallas kernels: 2.82 us -> 14.6 us  [shards(): pl.pallas_call(functools.partial(place_kernel, owners), out_shape=(jax.Sh...]
    unnamed x4 -> x0, local copies, waits for them, and re-layouts: 5.72 us -> none
    pallas_call x1, Pallas kernels: 36.8 us -> 35.7 us  [shards(): pl.pallas_call(functools.partial(exchange_kernel, owners, heads, sizes),...]
where the time goes in v2:
time: 51.1 us; the launch traced here: 50.9 us
  Pallas kernels  50.2 us (98%)
  between operations  0.64 us (1%)
    pallas_call x1, Pallas kernels, shards(): pl.pallas_call(functools.partial(exchange_kernel, owners, heads, sizes),...  35.7 us
    pallas_call x1, Pallas kernels, shards(): pl.pallas_call(functools.partial(place_kernel, owners), out_shape=(jax.Sh...  14.6 us

profile of v2, /device:TPU:0, one launch (start us, length us, event | category | flops | bytes accessed | tf_op | source)
XLA Modules:
  0.0 50.9 jit_solution(12079528463226218520)
XLA Ops:
  0.6 35.7 %exchange.1 = (bf16[8,32,576]{2,1,0:T(8,128)(2,1)}, bf16[4,32,576]{2,1,0:T(8,128)(2,1)}, bf16[4,32,128]{2,1,0:T(8,128)(2,1)}, bf16[8,16,128]{2,1,0:T(8,128)(2,1)}, f32[8,16]{1,0:T(8,128)}, /*index=5*/s32[8,128]{1,0:T(8,128)}) custom-call(bf16[8,32,576]{2,1,0:T(8,128)(2,1)} %q_hbm.1, bf16[8,32,512]{2,1,0:T(8,128)(2,1)} %g_hbm.1, ...), custom_call_target="tpu_custom_call" | custom-call | tf_op jit(solution)/shard_map/exchange/pallas_call | solution.py:489
  36.3 14.6 %place.1 = (f32[32,32,576]{2,1,0:T(8,128)}, f32[32,32,128]{2,1,0:T(8,128)}, bf16[8,32,576]{2,1,0:T(8,128)(2,1)}, bf16[8,16,128]{2,1,0:T(8,128)(2,1)}, f32[8,16]{1,0:T(8,128)}) custom-call(s32[8,128]{1,0:T(8,128)} %get-tuple-element.16.home_ref, bf16[4,32,576]{2,1,0:T(8,128)(2,1)} %get-tuple-element.17.lat_hbm, ...), custom_call_target="tpu_custom_call" | custom-call | tf_op jit(solution)/shard_map/place/pallas_call | solution.py:554

commit v3 on v2

--- a/solution.py
+++ b/solution.py
@@ -92,7 +92,11 @@
     others = (beside, across, opposite)
 
     def ctx_at(step):
-        return lax.rem(me_c + step + owners, owners)
+        found = me_c
+        for bit in range(shift):
+            if step >> bit & 1:
+                found = found + (1 << bit) * (1 - 2 * lax.rem(me_c // (1 << bit), 2))
+        return found
 
     def remote(src, dst, send_sem, recv_sem, **where):
         return pltpu.make_async_remote_copy(
@@ -185,7 +189,7 @@
                 rows.at[step, me_h],
                 row_s.at[step - 1],
                 row_r.at[step - 1],
-                ctx=ctx_at(-step),
+                ctx=ctx_at(step),
             )
         )
     send(hand_on(0, me_h, 0, across))
@@ -309,25 +313,6 @@
             )
         )
 
-    for kind in range(2):
-        for number, other in enumerate(others):
-            slot = part.at[other, kind]
-            remote(
-                slot, slot, part_s.at[kind, number], part_r.at[kind, number], head=other
-            ).wait_recv()
-
-    def total_of(kind, step):
-        found = part[0, kind, step]
-        for head in range(1, heads):
-            found = found + part[head, kind, step]
-        return found
-
-    logits = [
-        jnp.where(seen[step] > 0.5, total_of(1, step), SCORE_FLOOR) for step in range(owners)
-    ]
-    probs = softmax(logits)
-    logit_grads = [probs[step] - total_of(0, step) * (1.0 / HEADS) for step in range(owners)]
-
     for step in order:
         remote(
             glat.at[step, :, 0],
@@ -344,6 +329,25 @@
                 mid_lat.at[step], far_lat.at[step], mid_s.at[step], mid_r.at[step], head=across
             )
         )
+
+    for kind in range(2):
+        for number, other in enumerate(others):
+            slot = part.at[other, kind]
+            remote(
+                slot, slot, part_s.at[kind, number], part_r.at[kind, number], head=other
+            ).wait_recv()
+
+    def total_of(kind, step):
+        found = part[0, kind, step]
+        for head in range(1, heads):
+            found = found + part[head, kind, step]
+        return found
+
+    logits = [
+        jnp.where(seen[step] > 0.5, total_of(1, step), SCORE_FLOOR) for step in range(owners)
+    ]
+    probs = softmax(logits)
+    logit_grads = [probs[step] - total_of(0, step) * (1.0 / HEADS) for step in range(owners)]
 
     spreads = []
     for step in range(owners):
@@ -561,7 +565,7 @@
             jax.ShapeDtypeStruct(index_weights.shape, full),
         ),
         in_specs=[pl.BlockSpec(memory_space=pltpu.SMEM)] + [anywhere] * 5,
-        out_specs=(vmem, vmem, anywhere, anywhere, anywhere),
+        out_specs=(vmem,) * 5,
         scratch_shapes=[
             pltpu.VMEM(back_lat.shape, low),
             pltpu.VMEM(back_key.shape, low),

time: 51.1 us -> 37.8 us (0.74)
  Pallas kernels: 50.2 us -> 36.9 us
    pallas_call x1, Pallas kernels: 14.6 us -> 3.62 us  [shards(): pl.pallas_call(functools.partial(place_kernel, owners), out_shape=(jax.Sh...]
    pallas_call x1, Pallas kernels: 35.7 us -> 33.3 us  [shards(): pl.pallas_call(functools.partial(exchange_kernel, owners, heads, sizes),...]
where the time goes in v3:
time: 37.8 us; the launch traced here: 37.6 us
  Pallas kernels  36.9 us (98%)
  between operations  0.64 us (2%)
    pallas_call x1, Pallas kernels, shards(): pl.pallas_call(functools.partial(exchange_kernel, owners, heads, sizes),...  33.3 us
    pallas_call x1, Pallas kernels, shards(): pl.pallas_call(functools.partial(place_kernel, owners), out_shape=(jax.Sh...  3.62 us

profile of v3, /device:TPU:0, one launch (start us, length us, event | category | flops | bytes accessed | tf_op | source)
XLA Modules:
  0.0 37.6 jit_solution(1037889336608963637)
XLA Ops:
  0.6 33.3 %exchange.1 = (bf16[8,32,576]{2,1,0:T(8,128)(2,1)}, bf16[4,32,576]{2,1,0:T(8,128)(2,1)}, bf16[4,32,128]{2,1,0:T(8,128)(2,1)}, bf16[8,16,128]{2,1,0:T(8,128)(2,1)}, f32[8,16]{1,0:T(8,128)}, /*index=5*/s32[8,128]{1,0:T(8,128)}) custom-call(bf16[8,32,576]{2,1,0:T(8,128)(2,1)} %q_hbm.1, bf16[8,32,512]{2,1,0:T(8,128)(2,1)} %g_hbm.1, ...), custom_call_target="tpu_custom_call" | custom-call | tf_op jit(solution)/shard_map/exchange/pallas_call | solution.py:493
  33.9 3.6 %place.1 = (f32[32,32,576]{2,1,0:T(8,128)}, f32[32,32,128]{2,1,0:T(8,128)}, bf16[8,32,576]{2,1,0:T(8,128)(2,1)}, bf16[8,16,128]{2,1,0:T(8,128)(2,1)}, f32[8,16]{1,0:T(8,128)}) custom-call(s32[8,128]{1,0:T(8,128)} %get-tuple-element.16.home_ref, bf16[4,32,576]{2,1,0:T(8,128)(2,1)} %get-tuple-element.17.lat_hbm, ...), custom_call_target="tpu_custom_call" | custom-call | tf_op jit(solution)/shard_map/place/pallas_call | solution.py:558

commit v4 on v3

--- a/solution.py
+++ b/solution.py
@@ -313,6 +313,11 @@
             )
         )
 
+    found = jnp.zeros((stack, key_width), jnp.float32)
+    for step in range(owners):
+        found = found + dot(score_grads[step], keys_of(step), NN)
+    qg_ref[...] = found.astype(jnp.bfloat16).reshape(row_count, local_heads, key_width)
+
     for step in order:
         remote(
             glat.at[step, :, 0],
@@ -367,11 +372,6 @@
             head=beside,
         )
     )
-    found = jnp.zeros((stack, key_width), jnp.float32)
-    for step in range(owners):
-        found = found + dot(score_grads[step], keys_of(step), NN)
-    qg_ref[...] = found.astype(jnp.bfloat16).reshape(row_count, local_heads, key_width)
-
     remote(
         gkey.at[:, :, 0], near_key, near_s.at[owners], near_r.at[owners], head=beside
     ).wait_recv()
@@ -432,8 +432,8 @@
 def place_kernel(
     owners,
     home_ref,
-    lat_hbm,
-    key_hbm,
+    lat_ref,
+    key_ref,
     qg_in,
     iqg_in,
     iwg_in,
@@ -444,31 +444,40 @@
     iwg_out,
     lat_buf,
     key_buf,
-    sems,
+    small_sem,
+    part_sem,
 ):
     copies = [
-        pltpu.make_async_copy(src, dst, sems.at[number])
+        pltpu.make_async_copy(src, dst, small_sem.at[number])
         for number, (src, dst) in enumerate(
-            (
-                (lat_hbm, lat_buf),
-                (key_hbm, key_buf),
-                (qg_in, qg_out),
-                (iqg_in, iqg_out),
-                (iwg_in, iwg_out),
-            )
+            ((qg_in, qg_out), (iqg_in, iqg_out), (iwg_in, iwg_out))
         )
     ]
     for copy in copies:
         copy.start()
-    lat_out[...] = jnp.zeros_like(lat_out)
-    key_out[...] = jnp.zeros_like(key_out)
-    copies[0].wait()
-    copies[1].wait()
-    for step in range(owners):
-        at = jnp.maximum(home_ref[0, step], 0)
-        lat_out[at] = lat_out[at] + lat_buf[step].astype(jnp.float32)
-        key_out[at] = key_out[at] + key_buf[step].astype(jnp.float32)
-    for copy in copies[2:]:
+    lane = lax.broadcasted_iota(jnp.int32, (1, LANES), 1)
+    told = home_ref[0:1, :]
+    homes = [jnp.max(jnp.where(lane == step, told, 0)) for step in range(owners)]
+    parts = part_sem.shape[1]
+    span = lat_buf.shape[0] // parts
+    for part in range(parts):
+        here = pl.ds(part * span, span)
+        lat_buf[here] = jnp.zeros((span, *lat_buf.shape[1:]), jnp.float32)
+        key_buf[here] = jnp.zeros((span, *key_buf.shape[1:]), jnp.float32)
+        for step in range(owners):
+            at = homes[step]
+
+            @pl.when((at >= part * span) & (at < (part + 1) * span))
+            def _():
+                lat_buf[at] = lat_buf[at] + lat_ref[step].astype(jnp.float32)
+                key_buf[at] = key_buf[at] + key_ref[step].astype(jnp.float32)
+
+        for kind, (buf, out) in enumerate(((lat_buf, lat_out), (key_buf, key_out))):
+            copies.append(
+                pltpu.make_async_copy(buf.at[here], out.at[here], part_sem.at[kind, part])
+            )
+            copies[-1].start()
+    for copy in copies:
         copy.wait()
 
 
@@ -493,12 +502,12 @@
     query_grad, back_lat, back_key, iquery_grad, weight_grad, home = pl.pallas_call(
         functools.partial(exchange_kernel, owners, heads, sizes),
         out_shape=(
-            jax.ShapeDtypeStruct(queries.shape, low),
-            jax.ShapeDtypeStruct((owners, shard_rows, key_width), low),
-            jax.ShapeDtypeStruct((owners, shard_rows, index_width), low),
-            jax.ShapeDtypeStruct(index_queries.shape, low),
-            jax.ShapeDtypeStruct(index_weights.shape, full),
-            jax.ShapeDtypeStruct((8, LANES), whole),
+            pltpu.VMEM(queries.shape, low),
+            pltpu.VMEM((owners, shard_rows, key_width), low),
+            pltpu.VMEM((owners, shard_rows, index_width), low),
+            pltpu.VMEM(index_queries.shape, low),
+            pltpu.VMEM(index_weights.shape, full),
+            pltpu.VMEM((8, LANES), whole),
         ),
         in_specs=[anywhere, anywhere, anywhere, anywhere, vmem, vmem, vmem, anywhere],
         out_specs=(vmem,) * 6,
@@ -564,16 +573,22 @@
             jax.ShapeDtypeStruct(index_queries.shape, low),
             jax.ShapeDtypeStruct(index_weights.shape, full),
         ),
-        in_specs=[pl.BlockSpec(memory_space=pltpu.SMEM)] + [anywhere] * 5,
-        out_specs=(vmem,) * 5,
+        in_specs=[vmem] * 6,
+        out_specs=(anywhere,) * 5,
         scratch_shapes=[
-            pltpu.VMEM(back_lat.shape, low),
-            pltpu.VMEM(back_key.shape, low),
-            sem((5,)),
+            pltpu.VMEM((own_count, shard_rows, key_width), full),
+            pltpu.VMEM((own_count, shard_rows, index_width), full),
+            sem((3,)),
+            sem((2, 4)),
         ],
         compiler_params=pltpu.CompilerParams(vmem_limit_bytes=VMEM_BYTES),
         name="place",
-    )(home, back_lat, back_key, query_grad, iquery_grad, weight_grad)
+    )(
+        *(
+            pltpu.with_memory_space_constraint(found, pltpu.VMEM)
+            for found in (home, back_lat, back_key, query_grad, iquery_grad, weight_grad)
+        )
+    )
     return (query_grad, latent_grad, iquery_grad, weight_grad, index_key_grad)
 
 

time: 37.8 us -> 35.2 us (0.931)
  Pallas kernels: 36.9 us -> 34.3 us
    pallas_call x1, Pallas kernels: 3.62 us -> 1.98 us  [shards(): pl.pallas_call(functools.partial(place_kernel, owners), out_shape=(jax.Sh...]
    pallas_call x1, Pallas kernels: 33.3 us -> 32.4 us  [shards(): pl.pallas_call(functools.partial(exchange_kernel, owners, heads, sizes),...]
where the time goes in v4:
time: 35.2 us; the launch traced here: 35 us
  Pallas kernels  34.3 us (97%)
  between operations  0.64 us (2%)
    pallas_call x1, Pallas kernels, shards(): pl.pallas_call(functools.partial(exchange_kernel, owners, heads, sizes),...  32.4 us
    pallas_call x1, Pallas kernels, shards(): pl.pallas_call(functools.partial(place_kernel, owners), out_shape=(jax.Sh...  1.98 us

profile of v4, /device:TPU:0, one launch (start us, length us, event | category | flops | bytes accessed | tf_op | source)
XLA Modules:
  0.0 35.0 jit_solution(3487882767360352835)
XLA Ops:
  0.6 32.4 %exchange.1 = (bf16[8,32,576]{2,1,0:T(8,128)(2,1)S(1)}, bf16[4,32,576]{2,1,0:T(8,128)(2,1)S(1)}, bf16[4,32,128]{2,1,0:T(8,128)(2,1)S(1)}, bf16[8,16,128]{2,1,0:T...) custom-call(bf16[8,32,576]{2,1,0:T(8,128)(2,1)} %q_hbm.1, bf16[8,32,512]{2,1,0:T(8,128)(2,1)} %g_hbm.1, ...), custom_call_target="tpu_custom_call" | custom-call | tf_op jit(solution)/shard_map/exchange/pallas_call | solution.py:502
  33.0 2.0 %place.1 = (f32[32,32,576]{2,1,0:T(8,128)}, f32[32,32,128]{2,1,0:T(8,128)}, bf16[8,32,576]{2,1,0:T(8,128)(2,1)}, bf16[8,16,128]{2,1,0:T(8,128)(2,1)}, f32[8,16]{1,0:T(8,128)}) custom-call(s32[8,128]{1,0:T(8,128)S(1)} %get-tuple-element.16.home_ref, bf16[4,32,576]{2,1,0:T(8,128)(2,1)S(1)} %get-tuple-element.17.lat_ref, ...), custom_call_target="tpu_custom_call" | custom-call | tf_op jit(solution)/shard_map/place/pallas_call | solution.py:567

commit v5 on v4

--- a/solution.py
+++ b/solution.py
@@ -31,9 +31,9 @@
     g_hbm,
     lat_hbm,
     key_hbm,
-    iq_ref,
-    iw_ref,
-    pick_ref,
+    iq_hbm,
+    iw_hbm,
+    pick_hbm,
     reach_hbm,
     qg_ref,
     back_lat_ref,
@@ -41,6 +41,9 @@
     iqg_ref,
     iwg_ref,
     home_ref,
+    iq_ref,
+    iw_ref,
+    pick_ref,
     q_buf,
     g_buf,
     lat_buf,
@@ -123,11 +126,12 @@
                 (reach_hbm, reach_buf),
                 (q_hbm, q_buf),
                 (g_hbm, g_buf),
+                (iq_hbm, iq_ref),
+                (iw_hbm, iw_ref),
+                (pick_hbm, pick_ref),
             )
         )
     ]
-    for load in loads:
-        load.start()
     barrier = pltpu.get_barrier_semaphore()
     for step in range(1, owners):
         pl.semaphore_signal(
@@ -135,6 +139,9 @@
         )
     for other in others:
         pl.semaphore_signal(barrier, inc=1, device_id={"head": other}, device_id_type=MESH)
+    for load in (loads[7], *loads[:7]):
+        load.start()
+    loads[7].wait()
 
     lane = lax.broadcasted_iota(jnp.int32, (row_count, LANES), 1)
     diagonal = lax.broadcasted_iota(
@@ -164,17 +171,21 @@
         )
         send(asks[-1])
 
-    def hand_on(step, slot_head, number, to):
-        slot = rows.at[step, slot_head]
-        return remote(slot, slot, fwd_s.at[step, number], fwd_r.at[step, number], head=to)
+    def hand_across(step, x):
+        slot = rows.at[step, x, my_core]
+        return remote(slot, slot, fwd_s.at[step, 0], fwd_r.at[step, 0], head=across)
+
+    def hand_beside(step, core):
+        slot = rows.at[step, :, core]
+        return remote(slot, slot, fwd_s.at[step, 1], fwd_r.at[step, 1], head=beside)
 
     loads[0].wait()
     loads[1].wait()
     first_lane = lax.broadcasted_iota(jnp.int32, (1, LANES), 1)
     own_round = jnp.max(jnp.where(first_lane == me_c, wanted, -1))
     at = jnp.maximum(own_round, 0)
-    rows[0, me_h, :, :key_width] = lat_buf[at]
-    rows[0, me_h, :, key_at:] = key_buf[at]
+    rows[0, my_x, my_core, :, :key_width] = lat_buf[at]
+    rows[0, my_x, my_core, :, key_at:] = key_buf[at]
     homes = [own_round]
     for step in range(1, owners):
         asks[step - 1].wait_recv()
@@ -186,14 +197,13 @@
         send(
             remote(
                 row_send.at[step - 1],
-                rows.at[step, me_h],
+                rows.at[step, my_x, my_core],
                 row_s.at[step - 1],
                 row_r.at[step - 1],
                 ctx=ctx_at(step),
             )
         )
-    send(hand_on(0, me_h, 0, across))
-    send(hand_on(0, me_h, 1, beside))
+    send(hand_across(0, my_x))
     home_lane = lax.broadcasted_iota(jnp.int32, home_ref.shape, 1)
     home_all = jnp.full(home_ref.shape, -1, jnp.int32)
     for step in range(owners):
@@ -216,8 +226,8 @@
         ok = used & (block * block_rows + offsets <= places) & (places < ends)
         seen.append(jnp.where(ok, 1.0, 0.0))
 
-    loads[3].wait()
-    loads[4].wait()
+    for load in loads[3:7]:
+        load.wait()
     stack = row_count * local_heads
     queries = q_buf[...].reshape(stack, key_width)
     grads = g_buf[...].reshape(stack, latent_width)
@@ -235,10 +245,10 @@
     index_scores, scores, pulls = [], [], []
 
     def keys_of(step):
-        return rows[step, :, :, :key_width].reshape(block_rows, key_width)
+        return rows[step, :, :, :, :key_width].reshape(block_rows, key_width)
 
     def ikeys_of(step):
-        return rows[step, :, :, key_at:].reshape(block_rows, index_width)
+        return rows[step, :, :, :, key_at:].reshape(block_rows, index_width)
 
     def multiply(step):
         found = dot(iqueries, ikeys_of(step), NT).reshape(row_count, index_heads, block_rows)
@@ -254,19 +264,17 @@
         if turn < owners and turn > 0:
             remote(
                 row_send.at[0],
-                rows.at[turn, me_h],
+                rows.at[turn, my_x, my_core],
                 row_s.at[turn - 1],
                 row_r.at[turn - 1],
                 ctx=ctx_at(turn),
             ).wait_recv()
-            send(hand_on(turn, me_h, 0, across))
-            send(hand_on(turn, me_h, 1, beside))
+            send(hand_across(turn, my_x))
         if 1 <= turn <= owners:
-            hand_on(turn - 1, across, 0, across).wait_recv()
-            send(hand_on(turn - 1, across, 2, beside))
+            hand_across(turn - 1, 1 - my_x).wait_recv()
+            send(hand_beside(turn - 1, my_core))
         if turn >= 2:
-            hand_on(turn - 2, beside, 1, beside).wait_recv()
-            hand_on(turn - 2, opposite, 2, beside).wait_recv()
+            hand_beside(turn - 2, 1 - my_core).wait_recv()
             multiply(turn - 2)
 
     def share(kind):
@@ -289,7 +297,24 @@
     share(0)
     inner = functools.reduce(jnp.add, [a * p for a, p in zip(attention, pulls)])
     inner = jnp.sum(inner, axis=-1, keepdims=True)
-    order = [*range(1, owners), 0]
+    order = [first + more for first in range(owners - 2, -1, -2) for more in range(2)]
+
+    def near_copy(first):
+        two = pl.ds(first, 2)
+        return remote(
+            glat.at[two, :, 1 - my_core],
+            near_lat.at[two],
+            near_s.at[first],
+            near_r.at[first],
+            head=beside,
+        )
+
+    def mid_copy(first):
+        two = pl.ds(first, 2)
+        return remote(
+            mid_lat.at[two], far_lat.at[two], mid_s.at[first], mid_r.at[first], head=across
+        )
+
     score_grads = [None] * owners
     shape = (heads // 2, 2, shard_rows)
     for step in order:
@@ -303,15 +328,8 @@
         glat[step, :, :, :, :latent_width] = front.reshape(*shape, latent_width)
         rest = key_grad[:, latent_width:].astype(jnp.bfloat16)
         glat[step, :, :, :, latent_width:] = rest.reshape(*shape, key_width - latent_width)
-        send(
-            remote(
-                glat.at[step, :, 1 - my_core],
-                near_lat.at[step],
-                near_s.at[step],
-                near_r.at[step],
-                head=beside,
-            )
-        )
+        if step % 2:
+            send(near_copy(step - 1))
 
     found = jnp.zeros((stack, key_width), jnp.float32)
     for step in range(owners):
@@ -319,21 +337,13 @@
     qg_ref[...] = found.astype(jnp.bfloat16).reshape(row_count, local_heads, key_width)
 
     for step in order:
-        remote(
-            glat.at[step, :, 0],
-            near_lat.at[step],
-            near_s.at[step],
-            near_r.at[step],
-            head=beside,
-        ).wait_recv()
+        if step % 2 == 0:
+            near_copy(step).wait_recv()
         total = glat[step, 1 - my_x, my_core].astype(jnp.float32)
         total = total + near_lat[step, 1 - my_x].astype(jnp.float32)
         mid_lat[step] = total.astype(jnp.bfloat16)
-        send(
-            remote(
-                mid_lat.at[step], far_lat.at[step], mid_s.at[step], mid_r.at[step], head=across
-            )
-        )
+        if step % 2:
+            send(mid_copy(step - 1))
 
     for kind in range(2):
         for number, other in enumerate(others):
@@ -415,9 +425,8 @@
             send(home_copy(*home, step))
 
     for step in order:
-        remote(
-            mid_lat.at[step], far_lat.at[step], mid_s.at[step], mid_r.at[step], head=across
-        ).wait_recv()
+        if step % 2 == 0:
+            mid_copy(step).wait_recv()
         send_home(glat, near_lat, far_lat, lat_home, step)
     remote(mid_key, far_key, mid_s.at[owners], mid_r.at[owners], head=across).wait_recv()
     for step in order:
@@ -509,9 +518,12 @@
             pltpu.VMEM(index_weights.shape, full),
             pltpu.VMEM((8, LANES), whole),
         ),
-        in_specs=[anywhere, anywhere, anywhere, anywhere, vmem, vmem, vmem, anywhere],
+        in_specs=[anywhere] * 8,
         out_specs=(vmem,) * 6,
         scratch_shapes=[
+            pltpu.VMEM(index_queries.shape, low),
+            pltpu.VMEM(index_weights.shape, full),
+            pltpu.VMEM(picked_blocks.shape[::-1], whole),
             pltpu.VMEM(queries.shape, low),
             pltpu.VMEM(out_grad.shape, low),
             pltpu.VMEM(latents.shape, low),
@@ -520,7 +532,7 @@
             pltpu.VMEM((8, LANES), whole),
             pltpu.VMEM((side, 8, LANES), whole),
             pltpu.VMEM((side, shard_rows, wide), low),
-            pltpu.VMEM((owners, heads, shard_rows, wide), low),
+            pltpu.VMEM((owners, heads // 2, 2, shard_rows, wide), low),
             pltpu.VMEM((heads, 2, owners, row_count, block_rows), full),
             pltpu.VMEM((owners, heads // 2, 2, shard_rows, key_width), low),
             pltpu.VMEM((owners, heads // 2, 2, shard_rows, index_width), low),
@@ -532,13 +544,13 @@
             pltpu.VMEM((owners, shard_rows, index_width), low),
             pltpu.VMEM((side, shard_rows, key_width), low),
             pltpu.VMEM((side, shard_rows, index_width), low),
-            sem((5,)),
-            sem((side,)),
-            sem((side,)),
-            sem((side,)),
-            sem((side,)),
-            sem((owners, 3)),
-            sem((owners, 3)),
+            sem((8,)),
+            sem((side,)),
+            sem((side,)),
+            sem((side,)),
+            sem((side,)),
+            sem((owners, 2)),
+            sem((owners, 2)),
             sem((2, 3)),
             sem((2, 3)),
             sem((owners + 1,)),

time: 35.2 us -> 34.1 us (0.969)
  Pallas kernels: 34.3 us -> 33.3 us
    pallas_call x1, Pallas kernels: 32.4 us -> 31.3 us  [shards(): pl.pallas_call(functools.partial(exchange_kernel, owners, heads, sizes),...]
where the time goes in v5:
time: 34.1 us; the launch traced here: 34 us
  Pallas kernels  33.3 us (98%)
  between operations  0.64 us (2%)
    pallas_call x1, Pallas kernels, shards(): pl.pallas_call(functools.partial(exchange_kernel, owners, heads, sizes),...  31.3 us
    pallas_call x1, Pallas kernels, shards(): pl.pallas_call(functools.partial(place_kernel, owners), out_shape=(jax.Sh...  1.99 us

profile of v5, /device:TPU:0, one launch (start us, length us, event | category | flops | bytes accessed | tf_op | source)
XLA Modules:
  0.0 34.0 jit_solution(2894282887971786396)
XLA Ops:
  0.6 31.3 %exchange.1 = (bf16[8,32,576]{2,1,0:T(8,128)(2,1)S(1)}, bf16[4,32,576]{2,1,0:T(8,128)(2,1)S(1)}, bf16[4,32,128]{2,1,0:T(8,128)(2,1)S(1)}, bf16[8,16,128]{2,1,0:T...) custom-call(bf16[8,32,576]{2,1,0:T(8,128)(2,1)} %q_hbm.1, bf16[8,32,512]{2,1,0:T(8,128)(2,1)} %g_hbm.1, ...), custom_call_target="tpu_custom_call" | custom-call | tf_op jit(solution)/shard_map/exchange/pallas_call | solution.py:511
  32.0 2.0 %place.1 = (f32[32,32,576]{2,1,0:T(8,128)}, f32[32,32,128]{2,1,0:T(8,128)}, bf16[8,32,576]{2,1,0:T(8,128)(2,1)}, bf16[8,16,128]{2,1,0:T(8,128)(2,1)}, f32[8,16]{1,0:T(8,128)}) custom-call(s32[8,128]{1,0:T(8,128)S(1)} %get-tuple-element.16.home_ref, bf16[4,32,576]{2,1,0:T(8,128)(2,1)S(1)} %get-tuple-element.17.lat_ref, ...), custom_call_target="tpu_custom_call" | custom-call | tf_op jit(solution)/shard_map/place/pallas_call | solution.py:579

commit v6 on v5

--- a/solution.py
+++ b/solution.py
@@ -391,17 +391,6 @@
         mid_key[step] = total.astype(jnp.bfloat16)
     send(remote(mid_key, far_key, mid_s.at[owners], mid_r.at[owners], head=across))
 
-    found = jnp.zeros((index_stack, index_width), jnp.float32)
-    weight_grad = jnp.zeros((row_count, index_heads, block_rows), jnp.float32)
-    for step in range(owners):
-        found = found + dot(spreads[step], ikeys_of(step), NN)
-        weight_grad = weight_grad + logit_grads[step][:, None, :] * jnp.maximum(
-            index_scores[step], 0.0
-        )
-    iqg_ref[...] = found.astype(jnp.bfloat16).reshape(row_count, index_heads, index_width)
-    weight_grad = jnp.sum(weight_grad, axis=-1, keepdims=True)
-    iwg_ref[...] = jnp.sum(weight_grad * eye[None], axis=1)
-
     def home_copy(out, back_ref, out_s, out_r, step):
         return remote(
             out.at[step - 1],
@@ -424,7 +413,22 @@
             home[0][step - 1] = total
             send(home_copy(*home, step))
 
-    for step in order:
+    mid_copy(order[0]).wait_recv()
+    for step in order[:2]:
+        send_home(glat, near_lat, far_lat, lat_home, step)
+
+    found = jnp.zeros((index_stack, index_width), jnp.float32)
+    weight_grad = jnp.zeros((row_count, index_heads, block_rows), jnp.float32)
+    for step in range(owners):
+        found = found + dot(spreads[step], ikeys_of(step), NN)
+        weight_grad = weight_grad + logit_grads[step][:, None, :] * jnp.maximum(
+            index_scores[step], 0.0
+        )
+    iqg_ref[...] = found.astype(jnp.bfloat16).reshape(row_count, index_heads, index_width)
+    weight_grad = jnp.sum(weight_grad, axis=-1, keepdims=True)
+    iwg_ref[...] = jnp.sum(weight_grad * eye[None], axis=1)
+
+    for step in order[2:]:
         if step % 2 == 0:
             mid_copy(step).wait_recv()
         send_home(glat, near_lat, far_lat, lat_home, step)

time: 34.1 us -> 34.1 us (level)
  no operation moved by 1% of the time
where the time goes in v6:
time: 34.1 us; the launch traced here: 33.9 us
  Pallas kernels  33.3 us (98%)
  between operations  0.64 us (2%)
    pallas_call x1, Pallas kernels, shards(): pl.pallas_call(functools.partial(exchange_kernel, owners, heads, sizes),...  31.3 us
    pallas_call x1, Pallas kernels, shards(): pl.pallas_call(functools.partial(place_kernel, owners), out_shape=(jax.Sh...  1.97 us

profile of v6, /device:TPU:0, one launch (start us, length us, event | category | flops | bytes accessed | tf_op | source)
XLA Modules:
  0.0 33.9 jit_solution(5520856674888610311)
XLA Ops:
  0.6 31.3 %exchange.1 = (bf16[8,32,576]{2,1,0:T(8,128)(2,1)S(1)}, bf16[4,32,576]{2,1,0:T(8,128)(2,1)S(1)}, bf16[4,32,128]{2,1,0:T(8,128)(2,1)S(1)}, bf16[8,16,128]{2,1,0:T...) custom-call(bf16[8,32,576]{2,1,0:T(8,128)(2,1)} %q_hbm.1, bf16[8,32,512]{2,1,0:T(8,128)(2,1)} %g_hbm.1, ...), custom_call_target="tpu_custom_call" | custom-call | tf_op jit(solution)/shard_map/exchange/pallas_call | solution.py:515
  31.9 2.0 %place.1 = (f32[32,32,576]{2,1,0:T(8,128)}, f32[32,32,128]{2,1,0:T(8,128)}, bf16[8,32,576]{2,1,0:T(8,128)(2,1)}, bf16[8,16,128]{2,1,0:T(8,128)(2,1)}, f32[8,16]{1,0:T(8,128)}) custom-call(s32[8,128]{1,0:T(8,128)S(1)} %get-tuple-element.16.home_ref, bf16[4,32,576]{2,1,0:T(8,128)(2,1)S(1)} %get-tuple-element.17.lat_ref, ...), custom_call_target="tpu_custom_call" | custom-call | tf_op jit(solution)/shard_map/place/pallas_call | solution.py:583
